TPU v7x, 256 devices: a whole 4x4x8 slice. The times are simulated.
256 devices in a mesh: ctx: 32 (over z_lo, y, core), head: 8 (over x, z_hi).
Axes of the slice: x: 4, y: 4, z: 8 (z_hi: 2, z_lo: 4; z = z_hi * 4 + z_lo), core: 2. Of those that a mesh axis runs over, the one named last changes fastest.
Arguments:
- queries: bfloat16 [8192, 5120], P('ctx', 'head'), may hold values from -45 to 45, as said below
- keys: bfloat16 [8192, 1024], P('ctx', 'head'), may hold values from -6 to 6
- values: bfloat16 [8192, 1024], P('ctx', 'head'), may hold values from -6 to 6
- grad_out: bfloat16 [8192, 5120], P('ctx', 'head'), may hold values from -6 to 6
- w_query: bfloat16 [5120, 5120], P(None, 'head'), may hold values from -0.078125 to 0.078125
Outputs:
- grad_input: bfloat16 [8192, 5120], P('ctx', 'head')
- grad_keys: bfloat16 [8192, 1024], P('ctx', 'head')
- grad_values: bfloat16 [8192, 1024], P('ctx', 'head')
Inputs may be any that keep to these rules, and one draw needn't show every extreme that they name: queries of a few tokens may be large multiples of an earlier key.
All inputs are finite; a program needn't handle non-finite values.
Results may differ from a plain program's by a relative error of at most 0.025.
Values may be sent and summed in bfloat16 or wider, within the bound.
A program may use at most 128 MiB of HBM per device.

v0:
```python
import jax
import jax.numpy as jnp
from jax import lax
from jax.sharding import PartitionSpec as P

HD = 128


def local(queries, keys, values, grad_out, w_query):
    rows = queries.shape[0]
    kv_dev = keys.shape[1] // HD
    heads_dev = queries.shape[1] // HD
    group = heads_dev // kv_dev
    scale = HD ** (-0.5)
    my_index = lax.axis_index("ctx")
    ctx_count = lax.axis_size("ctx")
    first = my_index * rows
    final = first + rows - 1
    total_rows = rows * ctx_count
    q_group = (
        queries.reshape(rows, kv_dev, group, HD)
        .transpose(1, 2, 0, 3)
        .reshape(kv_dev, group * rows, HD)
    )
    o_group = (
        grad_out.reshape(rows, kv_dev, group, HD)
        .transpose(1, 2, 0, 3)
        .reshape(kv_dev, group * rows, HD)
    )
    q_pos = first + jnp.tile(jnp.arange(rows, dtype=jnp.int32), group)

    def split_heads(block):
        return block.reshape(block.shape[0], kv_dev, HD).transpose(1, 0, 2)

    def block_scores(key_blk, val_blk, key_start):
        key_pos = key_start + jnp.arange(key_blk.shape[1], dtype=jnp.int32)
        causal = key_pos[None, :] <= q_pos[:, None]
        scores = (
            jnp.einsum("kqd,ksd->kqs", q_group, key_blk, preferred_element_type=jnp.float32) * scale
        )
        dprobs = jnp.einsum("kqd,ksd->kqs", o_group, val_blk, preferred_element_type=jnp.float32)
        return (scores, dprobs, causal[None, :, :])

    def run_blocks(block_fn, carry, key_piece, val_piece):
        count = key_piece.shape[0]
        width = count
        while width > 1024 and width % 2 == 0:
            width = width // 2

        def advance(index, state):
            key_start = index * width
            key_blk = split_heads(lax.dynamic_slice_in_dim(key_piece, index * width, width, 0))
            val_blk = split_heads(lax.dynamic_slice_in_dim(val_piece, index * width, width, 0))
            return lax.cond(
                key_start <= final,
                lambda inner: block_fn(inner, key_blk, val_blk, key_start),
                lambda inner: inner,
                state,
            )

        return lax.fori_loop(0, count // width, advance, carry)

    def stats_block(state, key_blk, val_blk, key_start):
        running, totals, weighted = state
        scores, dprobs, causal = block_scores(key_blk, val_blk, key_start)
        scores = jnp.where(causal, scores, -1e30)
        updated = jnp.maximum(running, jnp.max(scores, axis=2))
        expo = jnp.where(causal, jnp.exp(scores - updated[:, :, None]), 0.0)
        factor = jnp.exp(running - updated)
        totals = totals * factor + jnp.sum(expo, axis=2)
        weighted = weighted * factor + jnp.sum(expo * dprobs, axis=2)
        return (updated, totals, weighted)

    stat_shape = (kv_dev, group * rows)
    stats_init = (
        jnp.full(stat_shape, -1e30, jnp.float32),
        jnp.zeros(stat_shape, jnp.float32),
        jnp.zeros(stat_shape, jnp.float32),
    )

    def block_grads(key_blk, val_blk, key_start, lse, delta):
        scores, dprobs, causal = block_scores(key_blk, val_blk, key_start)
        probs = jnp.where(causal, jnp.exp(scores - lse[:, :, None]), 0.0)
        probs_b = probs.astype(jnp.bfloat16)
        dscores = (probs * (dprobs - delta[:, :, None])).astype(jnp.bfloat16)
        q_term = jnp.einsum("kqs,ksd->kqd", dscores, key_blk, preferred_element_type=jnp.float32)
        key_term = (
            jnp.einsum("kqs,kqd->ksd", dscores, q_group, preferred_element_type=jnp.float32) * scale
        )
        val_term = jnp.einsum("kqs,kqd->ksd", probs_b, o_group, preferred_element_type=jnp.float32)
        both = (
            jnp.concatenate([key_term, val_term], axis=0)
            .transpose(1, 0, 2)
            .reshape(key_blk.shape[1], 2 * kv_dev * HD)
        )
        return (q_term, both)

    def grads_with(lse, delta):

        def grad_block(state, key_blk, val_blk, key_start):
            q_accum, kv_buffer = state
            q_term, both = block_grads(key_blk, val_blk, key_start, lse, delta)
            kv_buffer = lax.dynamic_update_slice_in_dim(kv_buffer, both, key_start, 0)
            return (q_accum + q_term, kv_buffer)

        def grad_fold(state, pieces, start):
            return run_blocks(grad_block, state, pieces[0], pieces[1])

        return grad_fold

    pieces = (
        lax.all_gather(keys, "ctx", axis=0, tiled=True),
        lax.all_gather(values, "ctx", axis=0, tiled=True),
    )
    running, totals, weighted = run_blocks(stats_block, stats_init, pieces[0], pieces[1])
    lse = running + jnp.log(totals)
    delta = weighted / totals
    q_start = jnp.zeros((kv_dev, group * rows, HD), jnp.float32)
    grads_init = (q_start, jnp.zeros((total_rows, 2 * kv_dev * HD), jnp.float32))
    q_accum, kv_buffer = grads_with(lse, delta)(
        grads_init,
        (
            lax.all_gather(keys, "ctx", axis=0, tiled=True),
            lax.all_gather(values, "ctx", axis=0, tiled=True),
        ),
        jnp.int32(0),
    )
    summed = lax.psum_scatter(
        kv_buffer.astype(jnp.bfloat16), "ctx", scatter_dimension=0, tiled=True
    ).astype(jnp.float32)
    grad_keys = summed[:, : kv_dev * HD].astype(jnp.bfloat16)
    grad_values = summed[:, kv_dev * HD :].astype(jnp.bfloat16)
    grad_q = (q_accum * scale).astype(jnp.bfloat16)
    q_flat = (
        grad_q.reshape(kv_dev, group, rows, HD).transpose(2, 0, 1, 3).reshape(rows, heads_dev * HD)
    )
    partial_input = lax.dot_general(
        q_flat, w_query, (((1,), (1,)), ((), ())), preferred_element_type=jnp.float32
    )
    grad_input = lax.psum_scatter(
        partial_input.astype(jnp.bfloat16), "head", scatter_dimension=1, tiled=True
    )
    return (grad_input, grad_keys, grad_values)


def solution(mesh):
    return jax.shard_map(
        local,
        mesh=mesh,
        in_specs=(
            P("ctx", "head"),
            P("ctx", "head"),
            P("ctx", "head"),
            P("ctx", "head"),
            P(None, "head"),
        ),
        out_specs=(P("ctx", "head"), P("ctx", "head"), P("ctx", "head")),
        check_vma=False,
    )
```

profile of v0, /device:TPU:121, one launch (start us, length us, event | category | flops | bytes accessed | tf_op | source)
XLA Modules:
  0.0 514.5 jit_solution(8444930005412594473)
XLA Ops:
  11.4 57.9 %all-gather.3.cloned.1.call-done = bf16[8192,128]{1,0:T(8,128)(2,1)} async-done(((bf16[256,128]{1,0:T(8,128)(2,1)}), bf16[8192,128]{1,0:T(8,128)(2,1)}) %all-gather.3.cloned.1.call-update) | async-done | bytes 2097168 | tf_op jit(solution)/shard_map/all_gather | solution.py:123
  69.3 60.9 %all-gather.5.cloned.1.call-done = bf16[8192,128]{1,0:T(8,128)(2,1)} async-done(((bf16[256,128]{1,0:T(8,128)(2,1)}), bf16[8192,128]{1,0:T(8,128)(2,1)}) %all-gather.5.cloned.1.call-update) | async-done | bytes 2097168 | tf_op jit(solution)/shard_map/all_gather | solution.py:124
  130.2 47.2 %while.34 = (s32[]{:T(128)}, f32[1,1280]{1,0:T(1,128)S(1)}, f32[1,1280]{1,0:T(1,128)S(1)}, f32[1,1280]{1,0:T(1,128)S(1)}, s32[]{:T(128)}, /*index=5*/bf16[8192,1...) while((s32[]{:T(128)}, f32[1,1280]{1,0:T(1,128)S(1)}, ...), condition=%wide.region_6.7_spmd.clone, body=%wide.region_0.6_spmd.clone.sunk | while | flops 688134144 | bytes 17063240 | solution.py:61
  130.3 5.9 %conditional.6 = ((f32[1,1280]{1,0:T(1,128)S(1)}, f32[1,1280]{1,0:T(1,128)S(1)}, f32[1,1280]{1,0:T(1,128)S(1)})) conditional(s32[]{:T(128)} %convert_element_type.54, (f32[1,1280]{1,0:T(1,128)S(1)}, f32[1,1280]{1,0:T(1,128)S(1)}, f32[1,1280]{1,0:T(1,128)S(1)}) %tuple.105, (s32[]{:T(128)}, s32[]{:T(128)}, bf16[8192,128]{1,0:T(8,128)(2,1)}, ...), branch_computations={%region_1.0_spmd, %region_2.5_spmd} | conditional | flops 688134144 | bytes 17057874 | solution.py:54
  136.2 5.9 %conditional.6 = ((f32[1,1280]{1,0:T(1,128)S(1)}, f32[1,1280]{1,0:T(1,128)S(1)}, f32[1,1280]{1,0:T(1,128)S(1)})) conditional(s32[]{:T(128)} %convert_element_type.54, (f32[1,1280]{1,0:T(1,128)S(1)}, f32[1,1280]{1,0:T(1,128)S(1)}, f32[1,1280]{1,0:T(1,128)S(1)}) %tuple.105, (s32[]{:T(128)}, s32[]{:T(128)}, bf16[8192,128]{1,0:T(8,128)(2,1)}, ...), branch_computations={%region_1.0_spmd, %region_2.5_spmd} | conditional | flops 688134144 | bytes 17057874 | solution.py:54
  142.1 5.9 %conditional.6 = ((f32[1,1280]{1,0:T(1,128)S(1)}, f32[1,1280]{1,0:T(1,128)S(1)}, f32[1,1280]{1,0:T(1,128)S(1)})) conditional(s32[]{:T(128)} %convert_element_type.54, (f32[1,1280]{1,0:T(1,128)S(1)}, f32[1,1280]{1,0:T(1,128)S(1)}, f32[1,1280]{1,0:T(1,128)S(1)}) %tuple.105, (s32[]{:T(128)}, s32[]{:T(128)}, bf16[8192,128]{1,0:T(8,128)(2,1)}, ...), branch_computations={%region_1.0_spmd, %region_2.5_spmd} | conditional | flops 688134144 | bytes 17057874 | solution.py:54
  148.0 5.9 %conditional.6 = ((f32[1,1280]{1,0:T(1,128)S(1)}, f32[1,1280]{1,0:T(1,128)S(1)}, f32[1,1280]{1,0:T(1,128)S(1)})) conditional(s32[]{:T(128)} %convert_element_type.54, (f32[1,1280]{1,0:T(1,128)S(1)}, f32[1,1280]{1,0:T(1,128)S(1)}, f32[1,1280]{1,0:T(1,128)S(1)}) %tuple.105, (s32[]{:T(128)}, s32[]{:T(128)}, bf16[8192,128]{1,0:T(8,128)(2,1)}, ...), branch_computations={%region_1.0_spmd, %region_2.5_spmd} | conditional | flops 688134144 | bytes 17057874 | solution.py:54
  153.9 5.9 %conditional.6 = ((f32[1,1280]{1,0:T(1,128)S(1)}, f32[1,1280]{1,0:T(1,128)S(1)}, f32[1,1280]{1,0:T(1,128)S(1)})) conditional(s32[]{:T(128)} %convert_element_type.54, (f32[1,1280]{1,0:T(1,128)S(1)}, f32[1,1280]{1,0:T(1,128)S(1)}, f32[1,1280]{1,0:T(1,128)S(1)}) %tuple.105, (s32[]{:T(128)}, s32[]{:T(128)}, bf16[8192,128]{1,0:T(8,128)(2,1)}, ...), branch_computations={%region_1.0_spmd, %region_2.5_spmd} | conditional | flops 688134144 | bytes 17057874 | solution.py:54
  159.8 5.9 %conditional.6 = ((f32[1,1280]{1,0:T(1,128)S(1)}, f32[1,1280]{1,0:T(1,128)S(1)}, f32[1,1280]{1,0:T(1,128)S(1)})) conditional(s32[]{:T(128)} %convert_element_type.54, (f32[1,1280]{1,0:T(1,128)S(1)}, f32[1,1280]{1,0:T(1,128)S(1)}, f32[1,1280]{1,0:T(1,128)S(1)}) %tuple.105, (s32[]{:T(128)}, s32[]{:T(128)}, bf16[8192,128]{1,0:T(8,128)(2,1)}, ...), branch_computations={%region_1.0_spmd, %region_2.5_spmd} | conditional | flops 688134144 | bytes 17057874 | solution.py:54
  165.7 5.9 %conditional.6 = ((f32[1,1280]{1,0:T(1,128)S(1)}, f32[1,1280]{1,0:T(1,128)S(1)}, f32[1,1280]{1,0:T(1,128)S(1)})) conditional(s32[]{:T(128)} %convert_element_type.54, (f32[1,1280]{1,0:T(1,128)S(1)}, f32[1,1280]{1,0:T(1,128)S(1)}, f32[1,1280]{1,0:T(1,128)S(1)}) %tuple.105, (s32[]{:T(128)}, s32[]{:T(128)}, bf16[8192,128]{1,0:T(8,128)(2,1)}, ...), branch_computations={%region_1.0_spmd, %region_2.5_spmd} | conditional | flops 688134144 | bytes 17057874 | solution.py:54
  171.6 5.9 %conditional.6 = ((f32[1,1280]{1,0:T(1,128)S(1)}, f32[1,1280]{1,0:T(1,128)S(1)}, f32[1,1280]{1,0:T(1,128)S(1)})) conditional(s32[]{:T(128)} %convert_element_type.54, (f32[1,1280]{1,0:T(1,128)S(1)}, f32[1,1280]{1,0:T(1,128)S(1)}, f32[1,1280]{1,0:T(1,128)S(1)}) %tuple.105, (s32[]{:T(128)}, s32[]{:T(128)}, bf16[8192,128]{1,0:T(8,128)(2,1)}, ...), branch_computations={%region_1.0_spmd, %region_2.5_spmd} | conditional | flops 688134144 | bytes 17057874 | solution.py:54
  180.0 71.8 %while.35 = (s32[]{:T(128)}, f32[1,1280,128]{2,1,0:T(8,128)S(1)}, bf16[8192,256]{0,1:T(8,128)(2,1)}, s32[]{:T(128)}, bf16[8192,128]{1,0:T(8,128)(2,1)}, /*index=...) while((s32[]{:T(128)}, f32[1,1280,128]{2,1,0:T(8,128)S(1)}, ...), condition=%wide.region_10.11_spmd.clone, body=%wide.region_7.10_spmd.clone.sunk | while | flops 1688897792 | bytes 29692248 | solution.py:61
  180.0 8.9 %conditional.7 = ((f32[1,1280,128]{2,1,0:T(8,128)S(1)}, bf16[8192,256]{0,1:T(8,128)(2,1)})) conditional(s32[]{:T(128)} %convert_element_type.55, (f32[1,1280,128]{2,1,0:T(8,128)S(1)}, bf16[8192,256]{0,1:T(8,128)(2,1)}) %tuple.108, (s32[]{:T(128)}, s32[]{:T(128)}, bf16[8192,128]{1,0:T(8,128)(2,1)}, bf16[1,1280,128]{2,1,0:T(8,128)(2,1)S(1)}, ...), branch_computations={%region_8.8_spmd, %region_9.9_spmd} | conditional | flops 1688897792 | bytes 29686874 | solution.py:54
  188.9 8.9 %conditional.7 = ((f32[1,1280,128]{2,1,0:T(8,128)S(1)}, bf16[8192,256]{0,1:T(8,128)(2,1)})) conditional(s32[]{:T(128)} %convert_element_type.55, (f32[1,1280,128]{2,1,0:T(8,128)S(1)}, bf16[8192,256]{0,1:T(8,128)(2,1)}) %tuple.108, (s32[]{:T(128)}, s32[]{:T(128)}, bf16[8192,128]{1,0:T(8,128)(2,1)}, bf16[1,1280,128]{2,1,0:T(8,128)(2,1)S(1)}, ...), branch_computations={%region_8.8_spmd, %region_9.9_spmd} | conditional | flops 1688897792 | bytes 29686874 | solution.py:54
  197.9 9.0 %conditional.7 = ((f32[1,1280,128]{2,1,0:T(8,128)S(1)}, bf16[8192,256]{0,1:T(8,128)(2,1)})) conditional(s32[]{:T(128)} %convert_element_type.55, (f32[1,1280,128]{2,1,0:T(8,128)S(1)}, bf16[8192,256]{0,1:T(8,128)(2,1)}) %tuple.108, (s32[]{:T(128)}, s32[]{:T(128)}, bf16[8192,128]{1,0:T(8,128)(2,1)}, bf16[1,1280,128]{2,1,0:T(8,128)(2,1)S(1)}, ...), branch_computations={%region_8.8_spmd, %region_9.9_spmd} | conditional | flops 1688897792 | bytes 29686874 | solution.py:54
  206.9 9.0 %conditional.7 = ((f32[1,1280,128]{2,1,0:T(8,128)S(1)}, bf16[8192,256]{0,1:T(8,128)(2,1)})) conditional(s32[]{:T(128)} %convert_element_type.55, (f32[1,1280,128]{2,1,0:T(8,128)S(1)}, bf16[8192,256]{0,1:T(8,128)(2,1)}) %tuple.108, (s32[]{:T(128)}, s32[]{:T(128)}, bf16[8192,128]{1,0:T(8,128)(2,1)}, bf16[1,1280,128]{2,1,0:T(8,128)(2,1)S(1)}, ...), branch_computations={%region_8.8_spmd, %region_9.9_spmd} | conditional | flops 1688897792 | bytes 29686874 | solution.py:54
  215.8 9.0 %conditional.7 = ((f32[1,1280,128]{2,1,0:T(8,128)S(1)}, bf16[8192,256]{0,1:T(8,128)(2,1)})) conditional(s32[]{:T(128)} %convert_element_type.55, (f32[1,1280,128]{2,1,0:T(8,128)S(1)}, bf16[8192,256]{0,1:T(8,128)(2,1)}) %tuple.108, (s32[]{:T(128)}, s32[]{:T(128)}, bf16[8192,128]{1,0:T(8,128)(2,1)}, bf16[1,1280,128]{2,1,0:T(8,128)(2,1)S(1)}, ...), branch_computations={%region_8.8_spmd, %region_9.9_spmd} | conditional | flops 1688897792 | bytes 29686874 | solution.py:54
  224.8 9.0 %conditional.7 = ((f32[1,1280,128]{2,1,0:T(8,128)S(1)}, bf16[8192,256]{0,1:T(8,128)(2,1)})) conditional(s32[]{:T(128)} %convert_element_type.55, (f32[1,1280,128]{2,1,0:T(8,128)S(1)}, bf16[8192,256]{0,1:T(8,128)(2,1)}) %tuple.108, (s32[]{:T(128)}, s32[]{:T(128)}, bf16[8192,128]{1,0:T(8,128)(2,1)}, bf16[1,1280,128]{2,1,0:T(8,128)(2,1)S(1)}, ...), branch_computations={%region_8.8_spmd, %region_9.9_spmd} | conditional | flops 1688897792 | bytes 29686874 | solution.py:54
  233.8 9.0 %conditional.7 = ((f32[1,1280,128]{2,1,0:T(8,128)S(1)}, bf16[8192,256]{0,1:T(8,128)(2,1)})) conditional(s32[]{:T(128)} %convert_element_type.55, (f32[1,1280,128]{2,1,0:T(8,128)S(1)}, bf16[8192,256]{0,1:T(8,128)(2,1)}) %tuple.108, (s32[]{:T(128)}, s32[]{:T(128)}, bf16[8192,128]{1,0:T(8,128)(2,1)}, bf16[1,1280,128]{2,1,0:T(8,128)(2,1)S(1)}, ...), branch_computations={%region_8.8_spmd, %region_9.9_spmd} | conditional | flops 1688897792 | bytes 29686874 | solution.py:54
  242.8 9.0 %conditional.7 = ((f32[1,1280,128]{2,1,0:T(8,128)S(1)}, bf16[8192,256]{0,1:T(8,128)(2,1)})) conditional(s32[]{:T(128)} %convert_element_type.55, (f32[1,1280,128]{2,1,0:T(8,128)S(1)}, bf16[8192,256]{0,1:T(8,128)(2,1)}) %tuple.108, (s32[]{:T(128)}, s32[]{:T(128)}, bf16[8192,128]{1,0:T(8,128)(2,1)}, bf16[1,1280,128]{2,1,0:T(8,128)(2,1)S(1)}, ...), branch_computations={%region_8.8_spmd, %region_9.9_spmd} | conditional | flops 1688897792 | bytes 29686874 | solution.py:54
  252.0 5.1 convolution_convert_fusion
  259.9 6.4 %copy.25 = bf16[8192,256]{1,0:T(8,128)(2,1)} copy(bf16[8192,256]{0,1:T(8,128)(2,1)} %get-tuple-element.615) | data formatting | bytes 8388608 | tf_op jit(solution)/shard_map/while | solution.py:61
  266.3 91.9 %reduce-scatter.7.cloned.1.call-done = bf16[640,256]{1,0:T(8,128)(2,1)} async-done(((bf16[5120,256]{1,0:T(8,128)(2,1)}), bf16[640,256]{1,0:T(8,128)(2,1)}) %reduce-scatter.7.cloned.1.call-update) | async-done | bytes 327696
  360.0 146.4 %reduce-scatter.5.cloned.1.call-done = bf16[256,256]{1,0:T(8,128)(2,1)} async-done(((bf16[8192,256]{1,0:T(8,128)(2,1)}), bf16[256,256]{1,0:T(8,128)(2,1)}) %reduce-scatter.5.cloned.1.call-update) | async-done | bytes 131088 | tf_op jit(solution)/shard_map/reduce_scatter | solution.py:128
  (207 shorter events, 130.5 us)
Async XLA Ops:
  7.2 62.1 %all-gather.3.cloned.1.call-start = ((), (), s32[]{:S(2)}) async-start(), calls=%async_computation.2 | async-start | bytes 2162688 | tf_op jit(solution)/shard_map/all_gather | solution.py:123
  7.9 122.3 %all-gather.5.cloned.1.call-start = ((), (), s32[]{:S(2)}) async-start(), calls=%async_computation.3 | async-start | bytes 2162688 | tf_op jit(solution)/shard_map/all_gather | solution.py:124
  8.6 349.5 %reduce-scatter.7.cloned.1.call-start = ((), (), s32[]{:S(2)}) async-start(), calls=%async_computation.5 | async-start | bytes 2949120
  259.8 246.6 %reduce-scatter.5.cloned.1.call-start = ((), (), s32[]{:S(2)}) async-start(), calls=%async_computation.4 | async-start | bytes 4325376 | tf_op jit(solution)/shard_map/reduce_scatter | solution.py:128
Sparse Core Ops, SparseCore 0:
  9.9 59.3 all-gather.2
  71.1 59.0 all-gather.4
  259.9 98.1 reduce-scatter.6
  360.5 145.8 reduce-scatter.4
where the time goes:
time: 523 us; the launch traced here: 515 us
  waiting for transfers between devices  358 us (68%)
  matrix products  102 us (20%)
  local copies, waits for them, and re-layouts  24.9 us (5%)
  between operations  13.8 us (3%)
  other arithmetic  13.2 us (3%)
    reduce_scatter x1, waiting for transfers between devices, local(): lax.psum_scatter(kv_buffer.astype(jnp.bfloat16), 'ctx', scatter_dimension...  146 us
    unnamed x5, waiting for transfers between devices  93.3 us
    all_gather x1, waiting for transfers between devices, local(): lax.all_gather(values, 'ctx', axis=0, tiled=True)  60.9 us
    all_gather x1, waiting for transfers between devices, local(): lax.all_gather(keys, 'ctx', axis=0, tiled=True)  57.9 us
    dot_general x16, matrix products, block_scores(): jnp.einsum('kqd,ksd->kqs', o_group, val_blk, preferred_element_type=jnp.f...  33.5 us
    dot_general x16, matrix products, block_scores(): jnp.einsum('kqd,ksd->kqs', q_group, key_blk, preferred_element_type=jnp.f...  32.7 us
    dot_general x8, matrix products, block_grads(): jnp.einsum('kqs,ksd->kqd', dscores, key_blk, preferred_element_type=jnp.f...  15.1 us
    reduce_sum x8, other arithmetic, stats_block(): totals = totals * factor + jnp.sum(expo, axis=2)  11.8 us
  transfers between devices with their start and end apart: 4, of which 4 were waited for; matrix products, arithmetic and copies ran while one was open for 2% of the time, Pallas kernels for 0%

commit v1 on v0

v1 whole, which is shorter than its diff:
```python
import functools

import jax
import jax.numpy as jnp
from jax import lax
from jax.experimental import pallas as pl
from jax.experimental.pallas import tpu as pltpu
from jax.sharding import PartitionSpec as P

HD = 128
B = 256
G = 5
R = G * B
NZ, NY, NK = 4, 4, 2
NX, NH = 4, 2
NB = NZ * NY * NK
ROW = NY * NK
COLS = G * HD
WIDE = NH * COLS
HALF = B // 2
SCALE = HD**-0.5
C = SCALE * 1.4426950408889634
NEG = -1e30
F32 = jnp.float32
BF = jnp.bfloat16
NT = (((1,), (1,)), ((), ()))
TN = (((0,), (0,)), ((), ()))
MESH = pl.DeviceIdType.MESH


def kernel(
    q_ref, k_ref, v_ref, o_ref, w_ref,
    gi_ref, gk_ref, gv_ref,
    kv, qa, oa, eb, db, ms, mr, lr, wr, dqt, dqb,
    ksta, ysta, zsta, zout, tot, s1, s2, hbuf,
    gz_s, gz_r, gy_s, gy_r, gk_s, gk_r,
    rk_s, rk_r, ry_s, ry_r, rz_s, rz_r,
    x1_s, x1_r, x2_s, x2_r, h_s, h_r, w_sem,
):
    ctx = lax.axis_index("ctx")
    head = lax.axis_index("head")
    k = lax.rem(ctx, NK)
    y = lax.rem(lax.div(ctx, NK), NY)
    z = lax.div(ctx, ROW)
    x = lax.div(head, NH)
    zh = lax.rem(head, NH)

    def at(zz, yy, kk):
        return ((zz * NY + yy) * NK + kk, head)

    def across(xx, hh):
        return (ctx, xx * NH + hh)

    def yp(d):
        return lax.rem(y + d, NY)

    def xp(d):
        return lax.rem(x + d, NX)

    sibling = at(z, y, 1 - k)
    up = at(jnp.minimum(z + 1, NZ - 1), y, k)
    down = at(jnp.maximum(z - 1, 0), y, k)

    def copy(src, dst, send, recv, to):
        return pltpu.make_async_remote_copy(
            src_ref=src, dst_ref=dst, send_sem=send, recv_sem=recv, device_id=to, device_id_type=MESH
        )

    def slot(row, yy, kk):
        return (row * NY + yy) * NK + kk

    kv[ctx, :, :HD] = k_ref[...]
    kv[ctx, :, HD:] = v_ref[...]
    for h in range(G):
        qa[h * B : (h + 1) * B, :] = q_ref[:, h * HD : (h + 1) * HD]
        oa[h * B : (h + 1) * B, :] = o_ref[:, h * HD : (h + 1) * HD]
    mr[...] = jnp.full_like(mr, NEG)
    lr[...] = jnp.zeros_like(lr)
    wr[...] = jnp.zeros_like(wr)

    barrier = pltpu.get_barrier_semaphore()

    def hello(to):
        pl.semaphore_signal(barrier, inc=1, device_id=to, device_id_type=MESH)

    hello(sibling)
    for d in range(1, NY):
        hello(at(z, yp(d), k))
    hello(across(xp(1), zh))
    hello(across(xp(NX - 1), zh))
    hello(across(x, 1 - zh))

    @pl.when(z < NZ - 1)
    def _():
        hello(up)

    @pl.when(z > 0)
    def _():
        hello(down)

    ends = jnp.where(z > 0, 1, 0) + jnp.where(z < NZ - 1, 1, 0)
    pl.semaphore_wait(barrier, NY + 3 + ends)

    def gather_z(s):
        b = kv.at[slot(z - s, y, k)]
        return copy(b, b, gz_s.at[s], gz_r.at[s + 1], up)

    def gather_z_in(s):
        b = kv.at[slot(z - s, y, k)]
        return copy(b, b, gz_s.at[s], gz_r.at[s], up)

    def gather_y(s, d):
        b = kv.at[slot(z - s, y, k)]
        return copy(b, b, gy_s.at[s, d - 1], gy_r.at[s, d - 1], at(z, yp(d), k))

    def gather_y_in(s, d):
        b = kv.at[slot(z - s, yp(NY - d), k)]
        return copy(b, b, gy_s.at[s, d - 1], gy_r.at[s, d - 1], at(z, yp(d), k))

    def gather_k(s, d):
        b = kv.at[slot(z - s, yp(NY - d), k)]
        return copy(b, b, gk_s.at[s, d], gk_r.at[s, d], sibling)

    def gather_k_in(s, d):
        b = kv.at[slot(z - s, yp(NY - d), 1 - k)]
        return copy(b, b, gk_s.at[s, d], gk_r.at[s, d], sibling)

    def gather_send(s):
        for d in (2, 1, 3):
            gather_y(s, d).start()

        @pl.when(z < NZ - 1)
        def _():
            gather_z(s).start()

        gather_k(s, 0).start()

    def gather_mid(s):
        for d in (1, 3, 2):
            gather_y_in(s, d).wait_recv()
            gather_k(s, d).start()

    def gather_end(s):
        for d in range(NY):
            gather_k_in(s, d).wait_recv()

    def first_block(j, masked):
        ks = pl.ds(pl.multiple_of(j * B, B), B)
        key = kv[j, :, :HD]
        val = kv[j, :, HD:]
        if masked:
            ok = lax.broadcasted_iota(jnp.int32, (B, B), 0) <= lax.broadcasted_iota(jnp.int32, (B, B), 1)
            ok3 = ok.reshape(B // 8, 8, B)
        for h in range(G):
            hs = slice(h * B, (h + 1) * B)
            s = lax.dot_general(key, qa[hs, :], NT, preferred_element_type=F32)
            t = lax.dot_general(val, oa[hs, :], NT, preferred_element_type=F32)
            if masked:
                s = jnp.where(ok, s, NEG)
            s3 = s.reshape(B // 8, 8, B)
            old = mr[:, hs]
            new = jnp.maximum(old, s3.max(0))
            e = jnp.exp2((s3 - new[None]) * C)
            if masked:
                e = jnp.where(ok3, e, 0.0)
            e_b = e.reshape(B, B).astype(BF)
            t_b = t.astype(BF)
            eb[ks, hs] = e_b
            db[ks, hs] = t_b
            e3 = e_b.astype(F32).reshape(B // 8, 8, B)
            t3 = t_b.astype(F32).reshape(B // 8, 8, B)
            f = jnp.exp2((old - new) * C)
            mr[:, hs] = new
            ms[j, :, hs] = new
            lr[:, hs] = lr[:, hs] * f + e3.sum(0)
            wr[:, hs] = wr[:, hs] * f + (e3 * t3).sum(0)

    def first_blocks(lo, hi):
        def body(j, _):
            first_block(j, False)
            return 0

        lax.fori_loop(lo, hi, body, 0)

    gather_send(0)
    first_block(ctx, True)
    gather_mid(0)
    gather_end(0)

    def first_row(s, _):
        base = (z - s) * ROW
        count = jnp.where(s == 0, ctx - z * ROW, ROW)
        half = lax.div(count, 2)

        @pl.when(s < z)
        def _():
            gather_z_in(s + 1).wait_recv()
            gather_send(s + 1)

        first_blocks(base, base + half)

        @pl.when(s < z)
        def _():
            gather_mid(s + 1)

        first_blocks(base + half, base + count)

        @pl.when(s < z)
        def _():
            gather_end(s + 1)

        return 0

    lax.fori_loop(0, z + 1, first_row, 0)

    def gather_sent(s, _):
        @pl.when(z < NZ - 1)
        def _():
            gather_z(s).wait_send()

        for d in range(1, NY):
            gather_y(s, d).wait_send()
        for d in range(NY):
            gather_k(s, d).wait_send()
        return 0

    lax.fori_loop(0, z + 1, gather_sent, 0)

    m8 = mr[...]
    top = m8.max(0, keepdims=True)
    f = jnp.exp2((m8 - top) * C)
    inv = 1.0 / (lr[...] * f).sum(0, keepdims=True)
    delta = (wr[...] * f).sum(0, keepdims=True) * inv
    mr[...] = jnp.broadcast_to(top, mr.shape)
    lr[...] = jnp.broadcast_to(inv, lr.shape)
    wr[...] = jnp.broadcast_to(delta, wr.shape)
    dqt[...] = jnp.zeros_like(dqt)

    def second_block(j, _):
        ks = pl.ds(pl.multiple_of(j * B, B), B)
        key = kv[j, :, :HD]
        dk = jnp.zeros((B, HD), F32)
        dv = jnp.zeros((B, HD), F32)
        for h in range(G):
            hs = slice(h * B, (h + 1) * B)
            f = jnp.exp2((ms[j, :, hs] - mr[:, hs]) * C) * lr[:, hs]
            p = eb[ks, hs].astype(F32).reshape(B // 8, 8, B) * f[None]
            ds = p * (db[ks, hs].astype(F32).reshape(B // 8, 8, B) - wr[:, hs][None])
            p_b = p.reshape(B, B).astype(BF)
            ds_b = ds.reshape(B, B).astype(BF)
            dv += jnp.dot(p_b, oa[hs, :], preferred_element_type=F32)
            dk += jnp.dot(ds_b, qa[hs, :], preferred_element_type=F32)
            dqt[:, hs] += lax.dot_general(key, ds_b, TN, preferred_element_type=F32)
        kv[j, :, :HD] = (dk * SCALE).astype(BF)
        kv[j, :, HD:] = dv.astype(BF)
        return 0

    def second_blocks(lo, hi):
        lax.fori_loop(lo, hi, second_block, 0)

    def sum_k(r, yy):
        return copy(kv.at[slot(r, yy, 1 - k)], ksta.at[r, yy], rk_s.at[r, yy], rk_r.at[r, yy], sibling)

    def sum_y(r, d):
        return copy(
            kv.at[slot(r, yp(d), k)], ysta.at[r, d - 1], ry_s.at[r, d - 1], ry_r.at[r, d - 1], at(z, yp(d), k)
        )

    def sum_z(r):
        return copy(zout.at[r], zsta.at[r], rz_s.at[r], rz_r.at[r], down)

    def sum_start(r):
        for yy in range(NY):
            sum_k(r, yy).start()

    def sum_mid(r):
        for yy in range(NY):
            sum_k(r, yy).wait_recv()
            b = slot(r, yy, k)
            kv[b] = (kv[b].astype(F32) + ksta[r, yy].astype(F32)).astype(BF)
        for d in (2, 1, 3):
            sum_y(r, d).start()

    def sum_row(r):
        t = kv[slot(r, y, k)].astype(F32)
        for d in range(1, NY):
            sum_y(r, d).wait_recv()
            t += ysta[r, d - 1].astype(F32)
        tot[r] = t

        @pl.when((z == NZ - 1) & (r < z))
        def _():
            zout[r] = t.astype(BF)
            sum_z(r).start()

    def fetch_w():
        return pltpu.make_async_copy(w_ref, eb.at[: NX * WIDE, :COLS], w_sem)

    def second_row(r, _):
        base = r * ROW
        count = jnp.where(r == z, ctx - z * ROW + 1, ROW)
        part = jnp.minimum(count, 2)

        @pl.when((r == z) & (z == NZ - 1))
        def _():
            fetch_w().start()

        second_blocks(base, base + part)

        @pl.when(r > 0)
        def _():
            sum_mid(r - 1)

        second_blocks(base + part, base + count)

        @pl.when(r > 0)
        def _():
            sum_row(r - 1)

        def clear(j, _):
            kv[j] = jnp.zeros((B, 2 * HD), BF)
            return 0

        lax.fori_loop(base + count, base + ROW, clear, 0)
        sum_start(r)
        return 0

    lax.fori_loop(0, z + 1, second_row, 0)

    @pl.when(z < NZ - 1)
    def _():
        fetch_w().start()

    for h in range(G):
        dqb[:, h * HD : (h + 1) * HD] = (dqt[:, h * B : (h + 1) * B] * SCALE).T.astype(BF)
    sum_mid(z)
    fetch_w().wait()

    def project(xx):
        out = lax.dot_general(
            dqb[...], eb[pl.ds(pl.multiple_of(xx * WIDE, WIDE), WIDE), :COLS], NT, preferred_element_type=F32
        )
        db[pl.ds(pl.multiple_of(xx * B, B), B), :] = out.astype(BF)

    def piece(xx, t, a):
        return db.at[pl.ds(pl.multiple_of(xx * B + t * HALF, HALF), HALF), a * COLS : (a + 1) * COLS]

    dx = (1, NX - 1)

    def two_away(t, a):
        return copy(piece(xp(2), t, a), s1.at[a, t], x1_s.at[a, t], x1_r.at[a, t], across(xp(dx[a]), zh))

    def next_to(t, way, a):
        return copy(
            piece(xp(dx[way]), t, a), s2.at[way, t, a], x2_s.at[way, t, a], x2_r.at[way, t, a],
            across(xp(dx[way]), zh),
        )

    def pass_on(t):
        for a in range(2):
            two_away(t, a).wait_recv()
            mine = piece(xp(dx[a]), t, a)
            mine[...] = (mine[...].astype(F32) + s1[a, t].astype(F32)).astype(BF)
            next_to(t, a, a).start()

    def z_half(t):
        return copy(hout(t), hbuf.at[t], h_s.at[t], h_r.at[t], across(x, 1 - zh))

    def hout(t):
        return db.at[pl.ds(NX * B + t * HALF, HALF), :COLS]

    def own_sum(t, a):
        out = piece(x, t, a)[...].astype(F32)
        for way in range(2):
            out += s2[way, t, a].astype(F32)
        return out

    project(xp(2))
    for t in range(2):
        for a in range(2):
            two_away(t, a).start()
    project(xp(1))
    next_to(0, 0, 1).start()
    project(xp(3))
    next_to(0, 1, 0).start()
    next_to(1, 0, 1).start()
    next_to(1, 1, 0).start()
    pass_on(0)
    project(x)
    pass_on(1)
    sum_row(z)

    for t in range(2):
        for way in range(2):
            for a in range(2):
                next_to(t, way, a).wait_recv()
        lo = own_sum(t, 0)
        hi = own_sum(t, 1)
        first = zh == 0
        hout(t)[...] = jnp.where(first, hi, lo).astype(BF)
        z_half(t).start()
        gi_ref[t * HALF : (t + 1) * HALF, :] = jnp.where(first, lo, hi).astype(BF)

    def chain(r, _):
        @pl.when(z < NZ - 1)
        def _():
            sum_z(r).wait_recv()
            tot[r] = tot[r] + zsta[r].astype(F32)

            @pl.when(r < z)
            def _():
                zout[r] = tot[r].astype(BF)
                sum_z(r).start()

        return 0

    lax.fori_loop(0, z + 1, chain, 0)
    gk_ref[...] = tot[z, :, :HD].astype(BF)
    gv_ref[...] = tot[z, :, HD:].astype(BF)

    for t in range(2):
        z_half(t).wait_recv()
        rows = slice(t * HALF, (t + 1) * HALF)
        gi_ref[rows, :] = (gi_ref[rows, :].astype(F32) + hbuf[t].astype(F32)).astype(BF)

    def sums_sent(r, _):
        for yy in range(NY):
            sum_k(r, yy).wait_send()
        for d in range(1, NY):
            sum_y(r, d).wait_send()

        @pl.when(r < z)
        def _():
            sum_z(r).wait_send()

        return 0

    lax.fori_loop(0, z + 1, sums_sent, 0)
    for t in range(2):
        for a in range(2):
            two_away(t, a).wait_send()
            for way in range(2):
                next_to(t, way, a).wait_send()
        z_half(t).wait_send()


def local(queries, keys, values, grad_out, w_query):
    dma = pltpu.SemaphoreType.DMA
    vm = pltpu.VMEM
    return pl.pallas_call(
        kernel,
        out_shape=(
            jax.ShapeDtypeStruct((B, COLS), BF),
            jax.ShapeDtypeStruct((B, HD), BF),
            jax.ShapeDtypeStruct((B, HD), BF),
        ),
        in_specs=[pl.BlockSpec(memory_space=pltpu.VMEM)] * 4 + [pl.BlockSpec(memory_space=pl.ANY)],
        out_specs=[pl.BlockSpec(memory_space=pltpu.VMEM)] * 3,
        scratch_shapes=[
            vm((NB, B, 2 * HD), BF),
            vm((R, HD), BF),
            vm((R, HD), BF),
            vm((NB * B, R), BF),
            vm((NB * B, R), BF),
            vm((NB, 8, R), F32),
            vm((8, R), F32),
            vm((8, R), F32),
            vm((8, R), F32),
            vm((HD, R), F32),
            vm((B, COLS), BF),
            vm((NZ, NY, B, 2 * HD), BF),
            vm((NZ, NY - 1, B, 2 * HD), BF),
            vm((NZ, B, 2 * HD), BF),
            vm((NZ, B, 2 * HD), BF),
            vm((NZ, B, 2 * HD), F32),
            vm((2, 2, HALF, COLS), BF),
            vm((2, 2, 2, HALF, COLS), BF),
            vm((2, HALF, COLS), BF),
            dma((NZ,)), dma((NZ + 1,)),
            dma((NZ, NY - 1)), dma((NZ, NY - 1)),
            dma((NZ, NY)), dma((NZ, NY)),
            dma((NZ, NY)), dma((NZ, NY)),
            dma((NZ, NY - 1)), dma((NZ, NY - 1)),
            dma((NZ,)), dma((NZ,)),
            dma((2, 2)), dma((2, 2)),
            dma((2, 2, 2)), dma((2, 2, 2)),
            dma((2,)), dma((2,)),
            dma(()),
        ],
        compiler_params=pltpu.CompilerParams(
            collective_id=0, has_side_effects=True, vmem_limit_bytes=62 * 1024 * 1024
        ),
    )(queries, keys, values, grad_out, w_query)


def solution(mesh):
    return jax.shard_map(
        local,
        mesh=mesh,
        in_specs=(
            P("ctx", "head"),
            P("ctx", "head"),
            P("ctx", "head"),
            P("ctx", "head"),
            P(None, "head"),
        ),
        out_specs=(P("ctx", "head"), P("ctx", "head"), P("ctx", "head")),
        check_vma=False,
    )
```

time: 523 us -> 131 us (0.25); the launches traced: 515 us -> 129 us
  waiting for transfers between devices: 358 us -> 0 us
  Pallas kernels: 0 us -> 124 us
  matrix products: 102 us -> 0 us
  local copies, waits for them, and re-layouts: 24.9 us -> 4.67 us
  other arithmetic: 13.2 us -> 0 us
  between operations: 13.8 us -> 0.64 us
    reduce_scatter x1 -> x0, waiting for transfers between devices: 146 us -> none  [local(): lax.psum_scatter(kv_buffer.astype(jnp.bfloat16), 'ctx', scatter_dimension...]
    pallas_call x0 -> x1, Pallas kernels: none -> 124 us  [local(): pl.pallas_call(kernel, out_shape=(jax.ShapeDtypeStruct((B, COLS), BF), ja...]
    all_gather x2 -> x0, waiting for transfers between devices: 119 us -> none  [the longest x1 60.9 us: local(): lax.all_gather(values, 'ctx', axis=0, tiled=True)]
    dot_general x57 -> x0, matrix products: 102 us -> none  [the longest x16 33.5 us: block_scores(): jnp.einsum('kqd,ksd->kqs', o_group, val_blk, preferred_element_type=jnp.f...]
    unnamed x5 -> x0, waiting for transfers between devices: 93.3 us -> none
    reduce_sum x8 -> x0, other arithmetic: 11.8 us -> none  [stats_block(): totals = totals * factor + jnp.sum(expo, axis=2)]
    dynamic_update_slice x8 -> x0, local copies, waits for them, and re-layouts: 6.98 us -> none  [grad_block(): kv_buffer = lax.dynamic_update_slice_in_dim(kv_buffer, both, key_start, 0)]
    while x1 -> x0, local copies, waits for them, and re-layouts: 6.39 us -> none  [run_blocks(): return lax.fori_loop(0, count // width, advance, carry)]
  transfers between devices with their start and end apart: 4 -> 0, of which waited for: 4 -> 0; matrix products, arithmetic and copies ran while one was open for 2% -> 0% of each run, Pallas kernels for 0% -> 0%
where the time goes in v1:
time: 131 us; the launch traced here: 129 us
  Pallas kernels  124 us (95%)
  local copies, waits for them, and re-layouts  4.67 us (4%)
    pallas_call x1, Pallas kernels, local(): pl.pallas_call(kernel, out_shape=(jax.ShapeDtypeStruct((B, COLS), BF), ja...  124 us
    unnamed x3, local copies, waits for them, and re-layouts  4.67 us

profile of v1, /device:TPU:121, one launch (start us, length us, event | category | flops | bytes accessed | tf_op | source)
XLA Modules:
  0.0 129.2 jit_solution(9415294395698999662)
XLA Ops:
  0.6 123.9 %shard_map.76 = (bf16[256,640]{1,0:T(8,128)(2,1)}, bf16[256,128]{1,0:T(8,128)(2,1)}, bf16[256,128]{1,0:T(8,128)(2,1)}) custom-call(bf16[256,640]{1,0:T(8,128)(2,1)} %q_ref.1, bf16[256,128]{1,0:T(8,128)(2,1)} %k_ref.1, bf16[256,128]{1,0:T(8,128)(2,1)} %v_ref.1, bf16[256,640]{1,0:T(8,128)(2,1)} %o_ref.1, bf16[5120,640]{1,0:T(8,128)(2,1)} %w_ref.1), custom_call_target="tpu_custom_call" | custom-call | tf_op jit(solution)/shard_map/pallas_call | solution.py:450
  124.5 1.7 %copy.11 = bf16[256,640]{1,0:T(8,128)(2,1)} copy(bf16[256,640]{1,0:T(8,128)(2,1)} %get-tuple-element.6) | data formatting | bytes 655360
  126.2 1.5 %copy.12 = bf16[256,128]{1,0:T(8,128)(2,1)} copy(bf16[256,128]{1,0:T(8,128)(2,1)} %get-tuple-element.7) | data formatting | bytes 131072
  127.7 1.5 %copy.13 = bf16[256,128]{1,0:T(8,128)(2,1)} copy(bf16[256,128]{1,0:T(8,128)(2,1)} %get-tuple-element.8) | data formatting | bytes 131072

commit v2 on v1

v2 whole, which is shorter than its diff:
```python
import functools

import jax
import jax.numpy as jnp
from jax import lax
from jax.experimental import pallas as pl
from jax.experimental.pallas import tpu as pltpu
from jax.sharding import PartitionSpec as P

HD = 128
B = 256
G = 5
R = G * B
NZ, NY, NK = 4, 4, 2
NX, NH = 4, 2
NB = NZ * NY * NK
ROW = NY * NK
COLS = G * HD
WIDE = NH * COLS
HALF = B // 2
T = G * HALF
MID = NX * WIDE
SCALE = HD**-0.5
C = SCALE * 1.4426950408889634
NEG = -1e30
F32 = jnp.float32
BF = jnp.bfloat16
NT = (((1,), (1,)), ((), ()))
TN = (((0,), (0,)), ((), ()))
MESH = pl.DeviceIdType.MESH


def kernel(
    q_ref, k_ref, v_ref, o_ref, w_ref,
    gi_ref, gk_ref, gv_ref,
    kv, qa, oa, eb, db, ms, mr, lr, wr, dqt, dqb,
    ksta, ysta, osta, zsta, zout, tot, s1, s2, hbuf, tail,
    g0_s, g0_r, gz_s, gz_r, gy_s, gy_r, gk_s, gk_r,
    rk_s, rk_r, ry_s, ry_r, ro_s, ro_r, rz_s, rz_r,
    x1_s, x1_r, x2_s, x2_r, h_s, h_r, w_sem,
):
    ctx = lax.axis_index("ctx")
    head = lax.axis_index("head")
    k = lax.rem(ctx, NK)
    y = lax.rem(lax.div(ctx, NK), NY)
    z = lax.div(ctx, ROW)
    x = lax.div(head, NH)
    zh = lax.rem(head, NH)

    def at(zz, yy, kk):
        return ((zz * NY + yy) * NK + kk, head)

    def across(xx, hh):
        return (ctx, xx * NH + hh)

    def yp(d):
        return lax.rem(y + d, NY)

    def xp(d):
        return lax.rem(x + d, NX)

    sibling = at(z, y, 1 - k)
    above = jnp.minimum(z + 1, NZ - 1)
    below = jnp.maximum(z - 1, 0)

    def copy(src, dst, send, recv, to):
        return pltpu.make_async_remote_copy(
            src_ref=src, dst_ref=dst, send_sem=send, recv_sem=recv, device_id=to, device_id_type=MESH
        )

    def slot(row, yy, kk):
        return (row * NY + yy) * NK + kk

    kv[ctx, :, :HD] = k_ref[...]
    kv[ctx, :, HD:] = v_ref[...]
    for t in range(2):
        for h in range(G):
            rows = slice(t * T + h * HALF, t * T + (h + 1) * HALF)
            qa[rows, :] = q_ref[t * HALF : (t + 1) * HALF, h * HD : (h + 1) * HD]
            oa[rows, :] = o_ref[t * HALF : (t + 1) * HALF, h * HD : (h + 1) * HD]
    mr[...] = jnp.full_like(mr, NEG)
    lr[...] = jnp.zeros_like(lr)
    wr[...] = jnp.zeros_like(wr)

    barrier = pltpu.get_barrier_semaphore()

    def hello(to):
        pl.semaphore_signal(barrier, inc=1, device_id=to, device_id_type=MESH)

    hello(sibling)
    for d in range(1, NY):
        hello(at(z, yp(d), k))
    hello(across(xp(1), zh))
    hello(across(xp(NX - 1), zh))
    hello(across(x, 1 - zh))

    @pl.when(z < NZ - 1)
    def _():
        hello(at(above, y, k))
        hello(at(above, yp(NY - 1), k))

    @pl.when(z > 0)
    def _():
        hello(at(below, y, k))
        hello(at(below, yp(1), k))

    ends = jnp.where(z > 0, 2, 0) + jnp.where(z < NZ - 1, 2, 0)
    pl.semaphore_wait(barrier, NY + 3 + ends)

    def block(s, j, kk):
        return kv.at[slot(z - s, yp(j), kk)]

    def own_y(d):
        b = block(0, 0, k)
        return copy(b, b, g0_s.at[d - 1], g0_r.at[d - 1], at(z, yp(d), k))

    def own_y_in(d):
        b = block(0, NY - d, k)
        return copy(b, b, g0_s.at[d - 1], g0_r.at[d - 1], at(z, yp(d), k))

    def own_z(i):
        b = block(0, 0, k)
        return copy(b, b, gz_s.at[0, i], gz_r.at[1, i], at(above, yp(NY - i), k))

    def gather_z(s, i):
        b = block(s, i, k)
        return copy(b, b, gz_s.at[s, i], gz_r.at[s + 1, i], at(above, y, k))

    def gather_z_in(s, i):
        b = block(s, i, k)
        return copy(b, b, gz_s.at[s, i], gz_r.at[s, i], at(above, y, k))

    def gather_y(s, i):
        b = block(s, i, k)
        return copy(b, b, gy_s.at[s, i], gy_r.at[s, i], at(z, yp((1, NY - 1)[i]), k))

    def gather_y_in(s, i):
        b = block(s, (NY - 1, 2)[i], k)
        return copy(b, b, gy_s.at[s, i], gy_r.at[s, i], at(z, yp((1, NY - 1)[i]), k))

    def gather_k(s, j):
        b = block(s, j, k)
        return copy(b, b, gk_s.at[s, j], gk_r.at[s, j], sibling)

    def gather_k_in(s, j):
        b = block(s, j, 1 - k)
        return copy(b, b, gk_s.at[s, j], gk_r.at[s, j], sibling)

    def own_send():
        for d in (1, 2, 3):
            @pl.when(y + d < NY)
            def _(d=d):
                own_y(d).start()

        @pl.when(k == 0)
        def _():
            gather_k(0, 0).start()

        @pl.when(z < NZ - 1)
        def _():
            own_z(0).start()
            own_z(1).start()

    def gather_up(s):
        for i in range(2):
            gather_z_in(s, i).wait_recv()

            @pl.when(z < NZ - 1)
            def _(i=i):
                gather_z(s, i).start()

            gather_y(s, i).start()
            gather_k(s, i).start()

    def first_block(j, masked):
        ks = pl.ds(pl.multiple_of(j * B, B), B)
        key = kv[j, :, :HD]
        val = kv[j, :, HD:]
        if masked:
            key_at = lax.broadcasted_iota(jnp.int32, (B, B), 0)
            col = lax.broadcasted_iota(jnp.int32, (B, B), 1)
        for h in range(G):
            hs = slice(h * B, (h + 1) * B)
            s = lax.dot_general(key, qa[hs, :], NT, preferred_element_type=F32)
            t = lax.dot_general(val, oa[hs, :], NT, preferred_element_type=F32)
            if masked:
                row = col + h * B
                ok = key_at <= lax.rem(row, HALF) + jnp.where(row >= T, HALF, 0)
                ok3 = ok.reshape(B // 8, 8, B)
                s = jnp.where(ok, s, NEG)
            s3 = s.reshape(B // 8, 8, B)
            old = mr[:, hs]
            new = jnp.maximum(old, s3.max(0))
            e = jnp.exp2((s3 - new[None]) * C)
            if masked:
                e = jnp.where(ok3, e, 0.0)
            e_b = e.reshape(B, B).astype(BF)
            t_b = t.astype(BF)
            eb[ks, hs] = e_b
            db[ks, hs] = t_b
            e3 = e_b.astype(F32).reshape(B // 8, 8, B)
            t3 = t_b.astype(F32).reshape(B // 8, 8, B)
            f = jnp.exp2((old - new) * C)
            mr[:, hs] = new
            ms[j, :, hs] = new
            lr[:, hs] = lr[:, hs] * f + e3.sum(0)
            wr[:, hs] = wr[:, hs] * f + (e3 * t3).sum(0)

    def first_two(a, b):
        def body(n, _):
            first_block(jnp.where(n == 0, a, b), False)
            return 0

        lax.fori_loop(0, 2, body, 0)

    own_send()
    first_block(ctx, True)

    @pl.when(k == 1)
    def _():
        gather_k_in(0, 0).wait_recv()
        first_block(ctx - 1, False)

    def own_step(d, _):
        @pl.when(d <= y)
        def _():
            own_y_in(d).wait_recv()
            gather_k(0, NY - d).start()
            first_block(slot(z, y - d, k), False)

        @pl.when((d == 1) & (z > 0))
        def _():
            gather_up(1)

        @pl.when(d <= y)
        def _():
            gather_k_in(0, NY - d).wait_recv()
            first_block(slot(z, y - d, 1 - k), False)

        return 0

    lax.fori_loop(1, jnp.maximum(y, 1) + 1, own_step, 0)

    def first_row(s, _):
        r = z - s
        first_two(slot(r, y, k), slot(r, yp(1), k))
        gather_k_in(s, 0).wait_recv()
        gather_k_in(s, 1).wait_recv()
        first_two(slot(r, y, 1 - k), slot(r, yp(1), 1 - k))
        for i in range(2):
            gather_y_in(s, i).wait_recv()
            gather_k(s, (NY - 1, 2)[i]).start()
        first_two(slot(r, yp(3), k), slot(r, yp(2), k))

        @pl.when(s < z)
        def _():
            gather_up(s + 1)

        gather_k_in(s, 3).wait_recv()
        gather_k_in(s, 2).wait_recv()
        first_two(slot(r, yp(3), 1 - k), slot(r, yp(2), 1 - k))
        return 0

    lax.fori_loop(1, z + 1, first_row, 0)

    @pl.when(z < NZ - 1)
    def _():
        own_z(0).wait_send()
        own_z(1).wait_send()

    for d in range(1, NY):
        @pl.when(y + d < NY)
        def _(d=d):
            own_y(d).wait_send()

        @pl.when(y >= d)
        def _(d=d):
            gather_k(0, NY - d).wait_send()

    @pl.when(k == 0)
    def _():
        gather_k(0, 0).wait_send()

    def gather_sent(s, _):
        for i in range(2):
            @pl.when(z < NZ - 1)
            def _(i=i):
                gather_z(s, i).wait_send()

            gather_y(s, i).wait_send()
        for j in range(NY):
            gather_k(s, j).wait_send()
        return 0

    lax.fori_loop(1, z + 1, gather_sent, 0)

    m8 = mr[...]
    top = m8.max(0, keepdims=True)
    f = jnp.exp2((m8 - top) * C)
    inv = 1.0 / (lr[...] * f).sum(0, keepdims=True)
    delta = (wr[...] * f).sum(0, keepdims=True) * inv
    mr[...] = jnp.broadcast_to(top, mr.shape)
    lr[...] = jnp.broadcast_to(inv, lr.shape)
    wr[...] = jnp.broadcast_to(delta, wr.shape)
    dqt[...] = jnp.zeros_like(dqt)

    def second_blocks(half, lo, hi):
        cuts = ((0, 2 * HD), (2 * HD, 4 * HD), (4 * HD, 5 * HD))

        def body(j, _):
            ks = pl.ds(pl.multiple_of(j * B, B), B)
            key = kv[j, :, :HD]
            dk = jnp.zeros((B, HD), F32)
            dv = jnp.zeros((B, HD), F32)
            for start, stop in cuts:
                hs = slice(half * T + start, half * T + stop)
                f = jnp.exp2((ms[j, :, hs] - mr[:, hs]) * C) * lr[:, hs]
                p = eb[ks, hs].astype(F32).reshape(B // 8, 8, stop - start) * f[None]
                ds = p * (db[ks, hs].astype(F32).reshape(B // 8, 8, stop - start) - wr[:, hs][None])
                p_b = p.reshape(B, stop - start).astype(BF)
                ds_b = ds.reshape(B, stop - start).astype(BF)
                dv += jnp.dot(p_b, oa[hs, :], preferred_element_type=F32)
                dk += jnp.dot(ds_b, qa[hs, :], preferred_element_type=F32)
                dqt[:, hs] += lax.dot_general(key, ds_b, TN, preferred_element_type=F32)
            dk = dk * SCALE
            if half == 0:
                db[ks, :HD] = dk.astype(BF)
                db[ks, HD : 2 * HD] = dv.astype(BF)
            else:
                kv[j, :, :HD] = (dk + db[ks, :HD].astype(F32)).astype(BF)
                kv[j, :, HD:] = (dv + db[ks, HD : 2 * HD].astype(F32)).astype(BF)
            return 0

        lax.fori_loop(lo, hi, body, 0)

    def sum_k(r, j):
        return copy(kv.at[slot(r, yp(j), 1 - k)], ksta.at[r, j], rk_s.at[r, j], rk_r.at[r, j], sibling)

    def sum_y(r, i):
        b = kv.at[slot(r, yp((NY - 1, 2)[i]), k)]
        return copy(b, ysta.at[r, i], ry_s.at[r, i], ry_r.at[r, i], at(z, yp((NY - 1, 1)[i]), k))

    def sum_z(r, i):
        yy = y if i == 0 else jnp.where(z == r + 1, yp(1), y)
        return copy(zout.at[r, i], zsta.at[r, i], rz_s.at[r, i], rz_r.at[r, i], at(below, yy, k))

    def sum_own(d):
        return copy(
            kv.at[slot(z, yp(NY - d), k)], osta.at[d - 1], ro_s.at[d - 1], ro_r.at[d - 1], at(z, yp(NY - d), k)
        )

    def add_k(r, j):
        sum_k(r, j).wait_recv()
        b = slot(r, yp(j), k)
        kv[b] = (kv[b].astype(F32) + ksta[r, j].astype(F32)).astype(BF)

    def sum_start(r):
        for j in (3, 2, 0, 1):
            sum_k(r, j).start()

    def sum_mid(r):
        add_k(r, 3)
        sum_y(r, 0).start()
        add_k(r, 2)
        sum_y(r, 1).start()
        add_k(r, 0)
        add_k(r, 1)

    def sum_row(r):
        for i in range(2):
            sum_y(r, i).wait_recv()
            t = kv[slot(r, yp(i), k)].astype(F32) + ysta[r, i].astype(F32)
            tot[r, i] = t

            @pl.when(z == NZ - 1)
            def _(i=i, t=t):
                zout[r, i] = t.astype(BF)
                sum_z(r, i).start()

    def own_start():
        for d in range(1, NY):
            @pl.when(y >= d)
            def _(d=d):
                sum_k(z, NY - d).start()

        @pl.when(k == 1)
        def _():
            sum_k(z, 0).start()

    def own_add():
        for d in range(1, NY):
            @pl.when(y >= d)
            def _(d=d):
                add_k(z, NY - d)
                sum_own(d).start()

        @pl.when(k == 0)
        def _():
            add_k(z, 0)

    def own_row():
        tot[z, 0] = kv[slot(z, y, k)].astype(F32)
        for d in range(1, NY):
            @pl.when(y + d < NY)
            def _(d=d):
                sum_own(d).wait_recv()
                tot[z, 0] = tot[z, 0] + osta[d - 1].astype(F32)

    def chain(r, here):
        @pl.when((z < NZ - 1) & (r < z) & here)
        def _():
            for i in range(2):
                sum_z(r, i).wait_recv()
                zout[r, i] = (tot[r, i] + zsta[r, i].astype(F32)).astype(BF)
                sum_z(r, i).start()

    def fetch_w():
        return pltpu.make_async_copy(w_ref, eb.at[:MID, :COLS], w_sem)

    dx = (1, NX - 1)

    def rows_of(t, xx, a):
        return pl.ds(pl.multiple_of(MID + t * (NX * NH + 2) * HALF + (xx * NH + a) * HALF, HALF), HALF)

    def piece(t, xx, a):
        return eb.at[rows_of(t, xx, a), :COLS]

    def project(t, xx):
        for a in range(NH):
            w = eb[pl.ds(pl.multiple_of(xx * WIDE + a * COLS, COLS), COLS), :COLS]
            out = lax.dot_general(dqb[t], w, NT, preferred_element_type=F32)
            eb[rows_of(t, xx, a), :COLS] = out.astype(BF)

    def two_away(t, a):
        return copy(piece(t, xp(2), a), s1.at[t, a], x1_s.at[t, a], x1_r.at[t, a], across(xp(dx[a]), zh))

    def next_to(t, way, a):
        return copy(
            piece(t, xp(dx[way]), a), s2.at[t, way, a], x2_s.at[t, way, a], x2_r.at[t, way, a],
            across(xp(dx[way]), zh),
        )

    def pass_on(t):
        for a in range(2):
            two_away(t, a).wait_recv()
            mine = piece(t, xp(dx[a]), a)
            mine[...] = (mine[...].astype(F32) + s1[t, a].astype(F32)).astype(BF)
            next_to(t, a, a).start()

    def z_last(t):
        return copy(piece(t, NX, 0), hbuf.at[t], h_s.at[t], h_r.at[t], across(x, 1 - zh))

    def own_sum(t, a):
        out = piece(t, x, a)[...].astype(F32)
        for way in range(2):
            out += s2[t, way, a].astype(F32)
        return out

    def arrived(t):
        for way in range(2):
            for a in range(2):
                next_to(t, way, a).wait_recv()
        lo = own_sum(t, 0)
        hi = own_sum(t, 1)
        first = zh == 0
        out = piece(t, NX, 0)
        out[...] = jnp.where(first, hi, lo).astype(BF)
        z_last(t).start()
        tail[t] = jnp.where(first, lo, hi)

    def finish(t):
        z_last(t).wait_recv()
        gi_ref[t * HALF : (t + 1) * HALF, :] = (tail[t] + hbuf[t].astype(F32)).astype(BF)

    def round_x(t, beside):
        for h in range(G):
            cols = slice(t * T + h * HALF, t * T + (h + 1) * HALF)
            dqb[t, :, h * HD : (h + 1) * HD] = (dqt[:, cols] * SCALE).T.astype(BF)
        project(t, xp(2))
        for a in range(2):
            two_away(t, a).start()
        beside()
        project(t, xp(1))
        next_to(t, 0, 1).start()
        project(t, xp(3))
        next_to(t, 1, 0).start()
        project(t, x)

    def nothing():
        pass

    second_blocks(0, 0, z * ROW)

    @pl.when(z == NZ - 1)
    def _():
        fetch_w().start()

    second_blocks(0, z * ROW, ctx + 1)

    @pl.when(z < NZ - 1)
    def _():
        fetch_w().start()

    fetch_w().wait()
    round_x(0, nothing)

    def second_row(r, _):
        base = r * ROW
        count = jnp.where(r == z, ctx - z * ROW + 1, ROW)
        part = jnp.minimum(count, 2)
        second_blocks(1, base, base + part)

        @pl.when(r > 0)
        def _():
            sum_mid(r - 1)

        second_blocks(1, base + part, base + count)

        @pl.when(r > 1)
        def _():
            sum_row(r - 2)

        @pl.when(r < z)
        def _():
            sum_start(r)

        @pl.when(r == jnp.minimum(z, 1))
        def _():
            pass_on(0)

        return 0

    lax.fori_loop(0, z + 1, second_row, 0)
    own_start()
    round_x(1, own_add)

    @pl.when(z > 0)
    def _():
        sum_row(z - 1)

    arrived(0)
    chain(0, z == NZ - 2)
    pass_on(1)
    own_row()
    arrived(1)
    for r in range(NZ - 1):
        chain(r, (z < NZ - 2) | (r > 0))

    @pl.when(z < NZ - 1)
    def _():
        for i in range(2):
            sum_z(z, i).wait_recv()
            tot[z, 0] = tot[z, 0] + zsta[z, i].astype(F32)

    gk_ref[...] = tot[z, 0, :, :HD].astype(BF)
    gv_ref[...] = tot[z, 0, :, HD:].astype(BF)
    finish(0)
    finish(1)

    def sums_sent(r, _):
        for j in range(NY):
            sum_k(r, j).wait_send()
        for i in range(2):
            sum_y(r, i).wait_send()
            sum_z(r, i).wait_send()
        return 0

    lax.fori_loop(0, z, sums_sent, 0)
    for d in range(1, NY):
        @pl.when(y >= d)
        def _(d=d):
            sum_k(z, NY - d).wait_send()
            sum_own(d).wait_send()

    @pl.when(k == 1)
    def _():
        sum_k(z, 0).wait_send()

    for t in range(2):
        for a in range(2):
            two_away(t, a).wait_send()
            for way in range(2):
                next_to(t, way, a).wait_send()
        z_last(t).wait_send()


def hand_out(*refs):
    moves = [pltpu.make_async_copy(refs[i], refs[6 + i], refs[9].at[i]) for i in range(3)]
    outs = [pltpu.make_async_copy(refs[6 + i], refs[3 + i], refs[9].at[i]) for i in range(3)]
    for move in moves:
        move.start()
    for move, out in zip(moves, outs):
        move.wait()
        out.start()
    for out in outs:
        out.wait()


def local(queries, keys, values, grad_out, w_query):
    dma = pltpu.SemaphoreType.DMA
    vm = pltpu.VMEM
    shapes = (
        jax.ShapeDtypeStruct((B, COLS), BF),
        jax.ShapeDtypeStruct((B, HD), BF),
        jax.ShapeDtypeStruct((B, HD), BF),
    )
    outs = pl.pallas_call(
        kernel,
        out_shape=shapes,
        in_specs=[pl.BlockSpec(memory_space=pltpu.VMEM)] * 4 + [pl.BlockSpec(memory_space=pl.ANY)],
        out_specs=[pl.BlockSpec(memory_space=pltpu.VMEM)] * 3,
        scratch_shapes=[
            vm((NB, B, 2 * HD), BF),
            vm((R, HD), BF),
            vm((R, HD), BF),
            vm((NB * B, R), BF),
            vm((NB * B, R), BF),
            vm((NB, 8, R), F32),
            vm((8, R), F32),
            vm((8, R), F32),
            vm((8, R), F32),
            vm((HD, R), F32),
            vm((2, HALF, COLS), BF),
            vm((NZ, NY, B, 2 * HD), BF),
            vm((NZ - 1, 2, B, 2 * HD), BF),
            vm((NY - 1, B, 2 * HD), BF),
            vm((NZ - 1, 2, B, 2 * HD), BF),
            vm((NZ - 1, 2, B, 2 * HD), BF),
            vm((NZ, 2, B, 2 * HD), F32),
            vm((2, 2, HALF, COLS), BF),
            vm((2, 2, 2, HALF, COLS), BF),
            vm((2, HALF, COLS), BF),
            vm((2, HALF, COLS), F32),
            dma((NY - 1,)), dma((NY - 1,)),
            dma((NZ, 2)), dma((NZ, 2)),
            dma((NZ, 2)), dma((NZ, 2)),
            dma((NZ, NY)), dma((NZ, NY)),
            dma((NZ, NY)), dma((NZ, NY)),
            dma((NZ - 1, 2)), dma((NZ - 1, 2)),
            dma((NY - 1,)), dma((NY - 1,)),
            dma((NZ - 1, 2)), dma((NZ - 1, 2)),
            dma((2, 2)), dma((2, 2)),
            dma((2, 2, 2)), dma((2, 2, 2)),
            dma((2,)), dma((2,)),
            dma(()),
        ],
        compiler_params=pltpu.CompilerParams(
            collective_id=0, has_side_effects=True, vmem_limit_bytes=62 * 1024 * 1024
        ),
    )(queries, keys, values, grad_out, w_query)
    return pl.pallas_call(
        hand_out,
        out_shape=shapes,
        in_specs=[pl.BlockSpec(memory_space=pl.ANY)] * 3,
        out_specs=[pl.BlockSpec(memory_space=pl.ANY)] * 3,
        scratch_shapes=[vm(a.shape, a.dtype) for a in shapes] + [dma((3,))],
    )(*outs)


def solution(mesh):
    return jax.shard_map(
        local,
        mesh=mesh,
        in_specs=(
            P("ctx", "head"),
            P("ctx", "head"),
            P("ctx", "head"),
            P("ctx", "head"),
            P(None, "head"),
        ),
        out_specs=(P("ctx", "head"), P("ctx", "head"), P("ctx", "head")),
        check_vma=False,
    )
```

time: 131 us -> 105 us (0.80)
  the two profiles are of different devices: /device:TPU:121 before, /device:TPU:32 now
where the time goes in v2:
time: 105 us; the launch traced here: 104 us
  Pallas kernels  104 us (99%)
    pallas_call x1, Pallas kernels, local(): pl.pallas_call(kernel, out_shape=shapes, in_specs=[pl.BlockSpec(memory_sp...  102 us

profile of v2, /device:TPU:32, one launch (start us, length us, event | category | flops | bytes accessed | tf_op | source)
XLA Modules:
  0.0 104.3 jit_solution(17711505387740975312)
XLA Ops:
  0.6 101.8 %shard_map.76 = (bf16[256,640]{1,0:T(8,128)(2,1)}, bf16[256,128]{1,0:T(8,128)(2,1)}, bf16[256,128]{1,0:T(8,128)(2,1)}) custom-call(bf16[256,640]{1,0:T(8,128)(2,1)} %q_ref.1, bf16[256,128]{1,0:T(8,128)(2,1)} %k_ref.1, bf16[256,128]{1,0:T(8,128)(2,1)} %v_ref.1, bf16[256,640]{1,0:T(8,128)(2,1)} %o_ref.1, bf16[5120,640]{1,0:T(8,128)(2,1)} %w_ref.1), custom_call_target="tpu_custom_call" | custom-call | tf_op jit(solution)/shard_map/pallas_call | solution.py:607
  102.4 1.8 %shard_map.77 = (bf16[256,640]{1,0:T(8,128)(2,1)}, bf16[256,128]{1,0:T(8,128)(2,1)}, bf16[256,128]{1,0:T(8,128)(2,1)}) custom-call(bf16[256,640]{1,0:T(8,128)(2,1)} %get-tuple-element.6.refs_0_, bf16[256,128]{1,0:T(8,128)(2,1)} %get-tuple-element.7.refs_1_, bf16[256,128]{1,0:T(8,128)(2,1)} %get-tuple-element.8.refs_2_), custom_call_target="tpu_custom_call" | custom-call | tf_op jit(solution)/shard_map/pallas_call | solution.py:651

commit v3 on v2

--- a/solution.py
+++ b/solution.py
@@ -15,6 +15,7 @@
 NX, NH = 4, 2
 NB = NZ * NY * NK
 ROW = NY * NK
+PAIR = NK * B
 COLS = G * HD
 WIDE = NH * COLS
 HALF = B // 2
@@ -34,10 +35,10 @@
     q_ref, k_ref, v_ref, o_ref, w_ref,
     gi_ref, gk_ref, gv_ref,
     kv, qa, oa, eb, db, ms, mr, lr, wr, dqt, dqb,
-    ksta, ysta, osta, zsta, zout, tot, s1, s2, hbuf, tail,
+    ksta, ysta, osta, zsta, tot, s1, s2, hbuf,
     g0_s, g0_r, gz_s, gz_r, gy_s, gy_r, gk_s, gk_r,
     rk_s, rk_r, ry_s, ry_r, ro_s, ro_r, rz_s, rz_r,
-    x1_s, x1_r, x2_s, x2_r, h_s, h_r, w_sem,
+    x1_s, x1_r, x2_s, x2_r, h_s, h_r, w_sem, in_sem,
 ):
     ctx = lax.axis_index("ctx")
     head = lax.axis_index("head")
@@ -71,13 +72,19 @@
     def slot(row, yy, kk):
         return (row * NY + yy) * NK + kk
 
-    kv[ctx, :, :HD] = k_ref[...]
-    kv[ctx, :, HD:] = v_ref[...]
+    def load(src, dst, n):
+        return pltpu.make_async_copy(src, dst, in_sem.at[n])
+
+    own_loads = [load(k_ref, kv.at[ctx, :, :HD], 0), load(v_ref, kv.at[ctx, :, HD:], 1)]
+    row_loads = []
     for t in range(2):
         for h in range(G):
-            rows = slice(t * T + h * HALF, t * T + (h + 1) * HALF)
-            qa[rows, :] = q_ref[t * HALF : (t + 1) * HALF, h * HD : (h + 1) * HD]
-            oa[rows, :] = o_ref[t * HALF : (t + 1) * HALF, h * HD : (h + 1) * HD]
+            at_rows = pl.ds(t * HALF, HALF), pl.ds(h * HD, HD)
+            to_rows = pl.ds(t * T + h * HALF, HALF)
+            row_loads.append(load(q_ref.at[at_rows], qa.at[to_rows], 2 + len(row_loads)))
+            row_loads.append(load(o_ref.at[at_rows], oa.at[to_rows], 2 + len(row_loads)))
+    for one in own_loads + row_loads:
+        one.start()
     mr[...] = jnp.full_like(mr, NEG)
     lr[...] = jnp.zeros_like(lr)
     wr[...] = jnp.zeros_like(wr)
@@ -152,114 +159,131 @@
             def _(d=d):
                 own_y(d).start()
 
-        @pl.when(k == 0)
-        def _():
-            gather_k(0, 0).start()
+        gather_k(0, 0).start()
 
         @pl.when(z < NZ - 1)
         def _():
             own_z(0).start()
             own_z(1).start()
 
-    def gather_up(s):
-        for i in range(2):
-            gather_z_in(s, i).wait_recv()
-
-            @pl.when(z < NZ - 1)
-            def _(i=i):
-                gather_z(s, i).start()
-
-            gather_y(s, i).start()
-            gather_k(s, i).start()
-
-    def first_block(j, masked):
-        ks = pl.ds(pl.multiple_of(j * B, B), B)
-        key = kv[j, :, :HD]
-        val = kv[j, :, HD:]
+    def gather_up(s, i):
+        gather_z_in(s, i).wait_recv()
+
+        @pl.when(z < NZ - 1)
+        def _():
+            gather_z(s, i).start()
+
+        gather_y(s, i).start()
+        gather_k(s, i).start()
+
+    def gather_over(s, i):
+        gather_y_in(s, i).wait_recv()
+        gather_k(s, (NY - 1, 2)[i]).start()
+
+    def first_pair(n, masked):
         if masked:
-            key_at = lax.broadcasted_iota(jnp.int32, (B, B), 0)
-            col = lax.broadcasted_iota(jnp.int32, (B, B), 1)
-        for h in range(G):
-            hs = slice(h * B, (h + 1) * B)
-            s = lax.dot_general(key, qa[hs, :], NT, preferred_element_type=F32)
-            t = lax.dot_general(val, oa[hs, :], NT, preferred_element_type=F32)
-            if masked:
-                row = col + h * B
-                ok = key_at <= lax.rem(row, HALF) + jnp.where(row >= T, HALF, 0)
-                ok3 = ok.reshape(B // 8, 8, B)
-                s = jnp.where(ok, s, NEG)
-            s3 = s.reshape(B // 8, 8, B)
-            old = mr[:, hs]
-            new = jnp.maximum(old, s3.max(0))
-            e = jnp.exp2((s3 - new[None]) * C)
-            if masked:
-                e = jnp.where(ok3, e, 0.0)
-            e_b = e.reshape(B, B).astype(BF)
-            t_b = t.astype(BF)
-            eb[ks, hs] = e_b
-            db[ks, hs] = t_b
-            e3 = e_b.astype(F32).reshape(B // 8, 8, B)
-            t3 = t_b.astype(F32).reshape(B // 8, 8, B)
-            f = jnp.exp2((old - new) * C)
-            mr[:, hs] = new
-            ms[j, :, hs] = new
-            lr[:, hs] = lr[:, hs] * f + e3.sum(0)
-            wr[:, hs] = wr[:, hs] * f + (e3 * t3).sum(0)
-
-    def first_two(a, b):
-        def body(n, _):
-            first_block(jnp.where(n == 0, a, b), False)
-            return 0
-
-        lax.fori_loop(0, 2, body, 0)
-
+            for lo in range(0, R, B):
+                first_part(n, masked, lo, B)
+        else:
+            first_part(n, masked, 0, R)
+
+    def first_part(n, masked, lo, W):
+        hs = slice(lo, lo + W)
+        ks = pl.ds(pl.multiple_of(n * PAIR, PAIR), PAIR)
+        both = kv[pl.ds(n * NK, NK)].reshape(PAIR, 2 * HD)
+        s = lax.dot_general(both[:, :HD], qa[hs, :], NT, preferred_element_type=F32)
+        t = lax.dot_general(both[:, HD:], oa[hs, :], NT, preferred_element_type=F32)
+        if masked:
+            key_at = lax.broadcasted_iota(jnp.int32, (PAIR, W), 0)
+            row = lax.broadcasted_iota(jnp.int32, (PAIR, W), 1) + lo
+            token = lax.rem(row, HALF) + jnp.where(row >= T, HALF, 0) + k * B
+            ok = key_at <= token
+            s = jnp.where(ok, s, NEG)
+        s3 = s.reshape(PAIR // 8, 8, W)
+        old = mr[:, hs]
+        new = jnp.maximum(old, s3.max(0))
+        e = jnp.exp2((s3 - new[None]) * C)
+        if masked:
+            e = jnp.where(ok.reshape(PAIR // 8, 8, W), e, 0.0)
+        t_b = t.astype(BF)
+        eb[ks, hs] = e.reshape(PAIR, W).astype(BF)
+        db[ks, hs] = t_b
+        f = jnp.exp2((old - new) * C)
+        mr[:, hs] = new
+        ms[n, :, hs] = new
+        lr[:, hs] = lr[:, hs] * f + e.sum(0)
+        wr[:, hs] = wr[:, hs] * f + (e * t_b.astype(F32).reshape(PAIR // 8, 8, W)).sum(0)
+
+    def pair(row, j):
+        return row * NY + yp(j)
+
+    for one in own_loads:
+        one.wait()
     own_send()
-    first_block(ctx, True)
-
-    @pl.when(k == 1)
-    def _():
-        gather_k_in(0, 0).wait_recv()
-        first_block(ctx - 1, False)
+    for one in row_loads:
+        one.wait()
+    gather_k_in(0, 0).wait_recv()
+    first_pair(pair(z, 0), True)
+
+    def own_in(d):
+        @pl.when(y >= d)
+        def _():
+            own_y_in(d).wait_recv()
+            gather_k(0, NY - d).start()
+
+    own_in(1)
+
+    @pl.when(z > 0)
+    def _():
+        gather_up(1, 0)
+
+    own_in(2)
 
     def own_step(d, _):
         @pl.when(d <= y)
         def _():
-            own_y_in(d).wait_recv()
-            gather_k(0, NY - d).start()
-            first_block(slot(z, y - d, k), False)
+            gather_k_in(0, NY - d).wait_recv()
+            first_pair(z * NY + y - d, False)
+
+        @pl.when(d == 1)
+        def _():
+            own_in(3)
 
         @pl.when((d == 1) & (z > 0))
         def _():
-            gather_up(1)
-
-        @pl.when(d <= y)
-        def _():
-            gather_k_in(0, NY - d).wait_recv()
-            first_block(slot(z, y - d, 1 - k), False)
+            gather_up(1, 1)
 
         return 0
 
     lax.fori_loop(1, jnp.maximum(y, 1) + 1, own_step, 0)
 
+    ready = jnp.where(z < NZ - 1, 0, 2)
+
     def first_row(s, _):
-        r = z - s
-        first_two(slot(r, y, k), slot(r, yp(1), k))
-        gather_k_in(s, 0).wait_recv()
-        gather_k_in(s, 1).wait_recv()
-        first_two(slot(r, y, 1 - k), slot(r, yp(1), 1 - k))
-        for i in range(2):
-            gather_y_in(s, i).wait_recv()
-            gather_k(s, (NY - 1, 2)[i]).start()
-        first_two(slot(r, yp(3), k), slot(r, yp(2), k))
-
-        @pl.when(s < z)
-        def _():
-            gather_up(s + 1)
-
-        gather_k_in(s, 3).wait_recv()
-        gather_k_in(s, 2).wait_recv()
-        first_two(slot(r, yp(3), 1 - k), slot(r, yp(2), 1 - k))
-        return 0
+        def step(n, _):
+            j = jnp.where(n == 2, 3, jnp.where(n == 3, 2, n))
+
+            @pl.when(n == 1)
+            def _():
+                gather_over(s, 0)
+
+            @pl.when(n == 2)
+            def _():
+                gather_over(s, 1)
+
+            @pl.when((n == ready) & (s < z))
+            def _():
+                gather_up(s + 1, 0)
+
+            @pl.when((n == ready + 1) & (s < z))
+            def _():
+                gather_up(s + 1, 1)
+
+            gather_k_in(s, j).wait_recv()
+            first_pair(pair(z - s, j), False)
+            return 0
+
+        return lax.fori_loop(0, NY, step, 0)
 
     lax.fori_loop(1, z + 1, first_row, 0)
 
@@ -277,9 +301,7 @@
         def _(d=d):
             gather_k(0, NY - d).wait_send()
 
-    @pl.when(k == 0)
-    def _():
-        gather_k(0, 0).wait_send()
+    gather_k(0, 0).wait_send()
 
     def gather_sent(s, _):
         for i in range(2):
@@ -304,34 +326,39 @@
     wr[...] = jnp.broadcast_to(delta, wr.shape)
     dqt[...] = jnp.zeros_like(dqt)
 
-    def second_blocks(half, lo, hi):
-        cuts = ((0, 2 * HD), (2 * HD, 4 * HD), (4 * HD, 5 * HD))
-
-        def body(j, _):
-            ks = pl.ds(pl.multiple_of(j * B, B), B)
-            key = kv[j, :, :HD]
-            dk = jnp.zeros((B, HD), F32)
-            dv = jnp.zeros((B, HD), F32)
-            for start, stop in cuts:
-                hs = slice(half * T + start, half * T + stop)
-                f = jnp.exp2((ms[j, :, hs] - mr[:, hs]) * C) * lr[:, hs]
-                p = eb[ks, hs].astype(F32).reshape(B // 8, 8, stop - start) * f[None]
-                ds = p * (db[ks, hs].astype(F32).reshape(B // 8, 8, stop - start) - wr[:, hs][None])
-                p_b = p.reshape(B, stop - start).astype(BF)
-                ds_b = ds.reshape(B, stop - start).astype(BF)
-                dv += jnp.dot(p_b, oa[hs, :], preferred_element_type=F32)
-                dk += jnp.dot(ds_b, qa[hs, :], preferred_element_type=F32)
-                dqt[:, hs] += lax.dot_general(key, ds_b, TN, preferred_element_type=F32)
-            dk = dk * SCALE
-            if half == 0:
-                db[ks, :HD] = dk.astype(BF)
-                db[ks, HD : 2 * HD] = dv.astype(BF)
-            else:
-                kv[j, :, :HD] = (dk + db[ks, :HD].astype(F32)).astype(BF)
-                kv[j, :, HD:] = (dv + db[ks, HD : 2 * HD].astype(F32)).astype(BF)
+    def second_pairs(half, first, count):
+        hs = slice(half * T, (half + 1) * T)
+        rows = count * PAIR
+        ks = pl.ds(pl.multiple_of(first * PAIR, PAIR), rows)
+        blocks = pl.ds(first * NK, count * NK)
+        p_b, ds_b = [], []
+        for i in range(count):
+            here = pl.ds(pl.multiple_of((first + i) * PAIR, PAIR), PAIR)
+            f = jnp.exp2((ms[first + i, :, hs] - mr[:, hs]) * C) * lr[:, hs]
+            p = eb[here, hs].astype(F32).reshape(PAIR // 8, 8, T) * f[None]
+            ds = p * (db[here, hs].astype(F32).reshape(PAIR // 8, 8, T) - wr[:, hs][None])
+            p_b.append(p.reshape(PAIR, T).astype(BF))
+            ds_b.append(ds.reshape(PAIR, T).astype(BF))
+        p_b = jnp.concatenate(p_b, axis=0)
+        ds_b = jnp.concatenate(ds_b, axis=0)
+        key = kv[blocks, :, :HD].reshape(rows, HD)
+        dv = jnp.dot(p_b, oa[hs, :], preferred_element_type=F32)
+        dk = jnp.dot(ds_b, qa[hs, :], preferred_element_type=F32) * SCALE
+        dqt[:, hs] += lax.dot_general(key, ds_b, TN, preferred_element_type=F32)
+        if half == 0:
+            db[ks, :HD] = dk.astype(BF)
+            db[ks, HD : 2 * HD] = dv.astype(BF)
+        else:
+            shape = (count * NK, B, HD)
+            kv[blocks, :, :HD] = (dk + db[ks, :HD].astype(F32)).astype(BF).reshape(shape)
+            kv[blocks, :, HD:] = (dv + db[ks, HD : 2 * HD].astype(F32)).astype(BF).reshape(shape)
+
+    def second_own(half):
+        def body(n, _):
+            second_pairs(half, z * NY + n, 1)
             return 0
 
-        lax.fori_loop(lo, hi, body, 0)
+        lax.fori_loop(0, y + 1, body, 0)
 
     def sum_k(r, j):
         return copy(kv.at[slot(r, yp(j), 1 - k)], ksta.at[r, j], rk_s.at[r, j], rk_r.at[r, j], sibling)
@@ -342,7 +369,7 @@
 
     def sum_z(r, i):
         yy = y if i == 0 else jnp.where(z == r + 1, yp(1), y)
-        return copy(zout.at[r, i], zsta.at[r, i], rz_s.at[r, i], rz_r.at[r, i], at(below, yy, k))
+        return copy(kv.at[slot(r, yp(i), k)], zsta.at[r, i], rz_s.at[r, i], rz_r.at[r, i], at(below, yy, k))
 
     def sum_own(d):
         return copy(
@@ -369,12 +396,11 @@
     def sum_row(r):
         for i in range(2):
             sum_y(r, i).wait_recv()
-            t = kv[slot(r, yp(i), k)].astype(F32) + ysta[r, i].astype(F32)
-            tot[r, i] = t
+            b = slot(r, yp(i), k)
+            kv[b] = (kv[b].astype(F32) + ysta[r, i].astype(F32)).astype(BF)
 
             @pl.when(z == NZ - 1)
-            def _(i=i, t=t):
-                zout[r, i] = t.astype(BF)
+            def _(i=i):
                 sum_z(r, i).start()
 
     def own_start():
@@ -399,19 +425,20 @@
             add_k(z, 0)
 
     def own_row():
-        tot[z, 0] = kv[slot(z, y, k)].astype(F32)
+        tot[...] = kv[slot(z, y, k)].astype(F32)
         for d in range(1, NY):
             @pl.when(y + d < NY)
             def _(d=d):
                 sum_own(d).wait_recv()
-                tot[z, 0] = tot[z, 0] + osta[d - 1].astype(F32)
-
-    def chain(r, here):
-        @pl.when((z < NZ - 1) & (r < z) & here)
+                tot[...] = tot[...] + osta[d - 1].astype(F32)
+
+    def chain(r):
+        @pl.when((z < NZ - 1) & (r < z))
         def _():
             for i in range(2):
                 sum_z(r, i).wait_recv()
-                zout[r, i] = (tot[r, i] + zsta[r, i].astype(F32)).astype(BF)
+                b = slot(r, yp(i), k)
+                kv[b] = (kv[b].astype(F32) + zsta[r, i].astype(F32)).astype(BF)
                 sum_z(r, i).start()
 
     def fetch_w():
@@ -466,11 +493,11 @@
         out = piece(t, NX, 0)
         out[...] = jnp.where(first, hi, lo).astype(BF)
         z_last(t).start()
-        tail[t] = jnp.where(first, lo, hi)
+        dqt[:, t * T : (t + 1) * T] = jnp.where(first, lo, hi)
 
     def finish(t):
         z_last(t).wait_recv()
-        gi_ref[t * HALF : (t + 1) * HALF, :] = (tail[t] + hbuf[t].astype(F32)).astype(BF)
+        gi_ref[t * HALF : (t + 1) * HALF, :] = (dqt[:, t * T : (t + 1) * T] + hbuf[t].astype(F32)).astype(BF)
 
     def round_x(t, beside):
         for h in range(G):
@@ -479,9 +506,9 @@
         project(t, xp(2))
         for a in range(2):
             two_away(t, a).start()
-        beside()
         project(t, xp(1))
         next_to(t, 0, 1).start()
+        beside()
         project(t, xp(3))
         next_to(t, 1, 0).start()
         project(t, x)
@@ -489,13 +516,17 @@
     def nothing():
         pass
 
-    second_blocks(0, 0, z * ROW)
+    def second_two(n, _):
+        second_pairs(0, 2 * n, 2)
+        return 0
+
+    lax.fori_loop(0, 2 * z, second_two, 0)
 
     @pl.when(z == NZ - 1)
     def _():
         fetch_w().start()
 
-    second_blocks(0, z * ROW, ctx + 1)
+    second_own(0)
 
     @pl.when(z < NZ - 1)
     def _():
@@ -505,55 +536,67 @@
     round_x(0, nothing)
 
     def second_row(r, _):
-        base = r * ROW
-        count = jnp.where(r == z, ctx - z * ROW + 1, ROW)
-        part = jnp.minimum(count, 2)
-        second_blocks(1, base, base + part)
+        def part(n, _):
+            second_pairs(1, r * NY + 2 * n, 2)
+            return 0
+
+        lax.fori_loop(0, 2, part, 0)
+        sum_start(r)
 
         @pl.when(r > 0)
         def _():
             sum_mid(r - 1)
 
-        second_blocks(1, base + part, base + count)
-
-        @pl.when(r > 1)
-        def _():
-            sum_row(r - 2)
-
-        @pl.when(r < z)
-        def _():
-            sum_start(r)
-
-        @pl.when(r == jnp.minimum(z, 1))
+        @pl.when(r == z - 1)
         def _():
             pass_on(0)
 
         return 0
 
-    lax.fori_loop(0, z + 1, second_row, 0)
+    lax.fori_loop(0, z, second_row, 0)
+    second_own(1)
     own_start()
-    round_x(1, own_add)
+
+    @pl.when(z == 0)
+    def _():
+        pass_on(0)
 
     @pl.when(z > 0)
     def _():
+        sum_mid(z - 1)
+
+    @pl.when(z > 1)
+    def _():
+        sum_row(0)
+
+    def between():
+        @pl.when(z > 2)
+        def _():
+            sum_row(1)
+
+        own_add()
+
+    round_x(1, between)
+
+    @pl.when(z > 0)
+    def _():
         sum_row(z - 1)
 
     arrived(0)
-    chain(0, z == NZ - 2)
     pass_on(1)
     own_row()
     arrived(1)
     for r in range(NZ - 1):
-        chain(r, (z < NZ - 2) | (r > 0))
+        chain(r)
 
     @pl.when(z < NZ - 1)
     def _():
         for i in range(2):
             sum_z(z, i).wait_recv()
-            tot[z, 0] = tot[z, 0] + zsta[z, i].astype(F32)
-
-    gk_ref[...] = tot[z, 0, :, :HD].astype(BF)
-    gv_ref[...] = tot[z, 0, :, HD:].astype(BF)
+            tot[...] = tot[...] + zsta[z, i].astype(F32)
+
+    gk_ref[...] = tot[:, :HD].astype(BF)
+    gv_ref[...] = tot[:, HD:].astype(BF)
     finish(0)
     finish(1)
 
@@ -607,7 +650,7 @@
     outs = pl.pallas_call(
         kernel,
         out_shape=shapes,
-        in_specs=[pl.BlockSpec(memory_space=pltpu.VMEM)] * 4 + [pl.BlockSpec(memory_space=pl.ANY)],
+        in_specs=[pl.BlockSpec(memory_space=pl.ANY)] * 5,
         out_specs=[pl.BlockSpec(memory_space=pltpu.VMEM)] * 3,
         scratch_shapes=[
             vm((NB, B, 2 * HD), BF),
@@ -615,7 +658,7 @@
             vm((R, HD), BF),
             vm((NB * B, R), BF),
             vm((NB * B, R), BF),
-            vm((NB, 8, R), F32),
+            vm((NB // NK, 8, R), F32),
             vm((8, R), F32),
             vm((8, R), F32),
             vm((8, R), F32),
@@ -625,12 +668,10 @@
             vm((NZ - 1, 2, B, 2 * HD), BF),
             vm((NY - 1, B, 2 * HD), BF),
             vm((NZ - 1, 2, B, 2 * HD), BF),
-            vm((NZ - 1, 2, B, 2 * HD), BF),
-            vm((NZ, 2, B, 2 * HD), F32),
+            vm((B, 2 * HD), F32),
             vm((2, 2, HALF, COLS), BF),
             vm((2, 2, 2, HALF, COLS), BF),
             vm((2, HALF, COLS), BF),
-            vm((2, HALF, COLS), F32),
             dma((NY - 1,)), dma((NY - 1,)),
             dma((NZ, 2)), dma((NZ, 2)),
             dma((NZ, 2)), dma((NZ, 2)),
@@ -643,9 +684,10 @@
             dma((2, 2, 2)), dma((2, 2, 2)),
             dma((2,)), dma((2,)),
             dma(()),
+            dma((2 + 4 * G,)),
         ],
         compiler_params=pltpu.CompilerParams(
-            collective_id=0, has_side_effects=True, vmem_limit_bytes=62 * 1024 * 1024
+            collective_id=0, has_side_effects=True, vmem_limit_bytes=65000000
         ),
     )(queries, keys, values, grad_out, w_query)
     return pl.pallas_call(

time: 105 us -> 93 us (0.89)
  the two profiles are of different devices: /device:TPU:32 before, /device:TPU:121 now
where the time goes in v3:
time: 93 us; the launch traced here: 92.8 us
  Pallas kernels  92.2 us (99%)
    pallas_call x1, Pallas kernels, local(): pl.pallas_call(kernel, out_shape=shapes, in_specs=[pl.BlockSpec(memory_sp...  90.4 us

profile of v3, /device:TPU:121, one launch (start us, length us, event | category | flops | bytes accessed | tf_op | source)
XLA Modules:
  0.0 92.8 jit_solution(5149804491557763185)
XLA Ops:
  0.6 90.4 %shard_map.76 = (bf16[256,640]{1,0:T(8,128)(2,1)}, bf16[256,128]{1,0:T(8,128)(2,1)}, bf16[256,128]{1,0:T(8,128)(2,1)}) custom-call(bf16[256,640]{1,0:T(8,128)(2,1)} %q_ref.1, bf16[256,128]{1,0:T(8,128)(2,1)} %k_ref.1, bf16[256,128]{1,0:T(8,128)(2,1)} %v_ref.1, bf16[256,640]{1,0:T(8,128)(2,1)} %o_ref.1, bf16[5120,640]{1,0:T(8,128)(2,1)} %w_ref.1), custom_call_target="tpu_custom_call" | custom-call | tf_op jit(solution)/shard_map/pallas_call | solution.py:650
  91.1 1.8 %shard_map.77 = (bf16[256,640]{1,0:T(8,128)(2,1)}, bf16[256,128]{1,0:T(8,128)(2,1)}, bf16[256,128]{1,0:T(8,128)(2,1)}) custom-call(bf16[256,640]{1,0:T(8,128)(2,1)} %get-tuple-element.6.refs_0_, bf16[256,128]{1,0:T(8,128)(2,1)} %get-tuple-element.7.refs_1_, bf16[256,128]{1,0:T(8,128)(2,1)} %get-tuple-element.8.refs_2_), custom_call_target="tpu_custom_call" | custom-call | tf_op jit(solution)/shard_map/pallas_call | solution.py:693

commit v4 on v3

--- a/solution.py
+++ b/solution.py
@@ -547,6 +547,10 @@
         def _():
             sum_mid(r - 1)
 
+        @pl.when(r > 1)
+        def _():
+            sum_row(r - 2)
+
         @pl.when(r == z - 1)
         def _():
             pass_on(0)
@@ -565,14 +569,10 @@
     def _():
         sum_mid(z - 1)
 
-    @pl.when(z > 1)
-    def _():
-        sum_row(0)
-
     def between():
-        @pl.when(z > 2)
-        def _():
-            sum_row(1)
+        @pl.when(z > 1)
+        def _():
+            sum_row(z - 2)
 
         own_add()
 

time: 93 us -> 92.5 us (level)
  no operation moved by 1% of the time
where the time goes in v4:
time: 92.5 us; the launch traced here: 92.1 us
  Pallas kernels  91.5 us (99%)
    pallas_call x1, Pallas kernels, local(): pl.pallas_call(kernel, out_shape=shapes, in_specs=[pl.BlockSpec(memory_sp...  89.7 us

profile of v4, /device:TPU:121, one launch (start us, length us, event | category | flops | bytes accessed | tf_op | source)
XLA Modules:
  0.0 92.1 jit_solution(2351367802275588654)
XLA Ops:
  0.6 89.7 %shard_map.76 = (bf16[256,640]{1,0:T(8,128)(2,1)}, bf16[256,128]{1,0:T(8,128)(2,1)}, bf16[256,128]{1,0:T(8,128)(2,1)}) custom-call(bf16[256,640]{1,0:T(8,128)(2,1)} %q_ref.1, bf16[256,128]{1,0:T(8,128)(2,1)} %k_ref.1, bf16[256,128]{1,0:T(8,128)(2,1)} %v_ref.1, bf16[256,640]{1,0:T(8,128)(2,1)} %o_ref.1, bf16[5120,640]{1,0:T(8,128)(2,1)} %w_ref.1), custom_call_target="tpu_custom_call" | custom-call | tf_op jit(solution)/shard_map/pallas_call | solution.py:650
  90.4 1.8 %shard_map.77 = (bf16[256,640]{1,0:T(8,128)(2,1)}, bf16[256,128]{1,0:T(8,128)(2,1)}, bf16[256,128]{1,0:T(8,128)(2,1)}) custom-call(bf16[256,640]{1,0:T(8,128)(2,1)} %get-tuple-element.6.refs_0_, bf16[256,128]{1,0:T(8,128)(2,1)} %get-tuple-element.7.refs_1_, bf16[256,128]{1,0:T(8,128)(2,1)} %get-tuple-element.8.refs_2_), custom_call_target="tpu_custom_call" | custom-call | tf_op jit(solution)/shard_map/pallas_call | solution.py:693
